TPU v7x, 128 devices: a whole 4x4x4 slice. The times are simulated.
128 devices in a mesh: seq: 8 (over z_hi, y), fsdp: 16 (over x, z_lo, core).
Axes of the slice: x: 4, y: 4, z: 4 (z_hi: 2, z_lo: 2; z = z_hi * 2 + z_lo), core: 2. Of those that a mesh axis runs over, the one named last changes fastest.
Arguments:
- hidden_in: bfloat16 [16, 1024, 2048], P('fsdp', 'seq'), may hold values from -6 to 6
- cotangent: bfloat16 [16, 1024, 2048], P('fsdp', 'seq'), may hold values from -6 to 6
- seq_lengths: int32 [16, 2], P('fsdp'), may hold values from 65 to 896, as said below
- slot_block: int32 [16, 8], P('fsdp'), may hold values from 0 to 7, as said below
- ln1_gain: bfloat16 [2048], P(('seq', 'fsdp')), may hold values from 0.25 to 1.75
- ln1_bias: bfloat16 [2048], P(('seq', 'fsdp')), may hold values from -1.1953125 to 1.1953125
- w_qkv: bfloat16 [2048, 6144], P(('seq', 'fsdp')), may hold values from -0.125 to 0.125
- qkv_bias: bfloat16 [6144], P(('seq', 'fsdp')), may hold values from -1.1953125 to 1.1953125
- w_out: bfloat16 [2048, 2048], P(('seq', 'fsdp')), may hold values from -0.5 to 0.5
- ln2_gain: bfloat16 [2048], P(('seq', 'fsdp')), may hold values from 0.25 to 1.75
- ln2_bias: bfloat16 [2048], P(('seq', 'fsdp')), may hold values from -1.1953125 to 1.1953125
- w_gate: bfloat16 [2048, 5632], P(('seq', 'fsdp')), may hold values from -0.125 to 0.125
- w_up: bfloat16 [2048, 5632], P(('seq', 'fsdp')), may hold values from -0.125 to 0.125
- w_down: bfloat16 [2048, 5632], P(('seq', 'fsdp')), may hold values from -0.078125 to 0.078125
Outputs:
- hidden_out: bfloat16 [16, 1024, 2048], P('fsdp', 'seq')
- input_grad: float32 [16, 1024, 2048], P('fsdp', 'seq')
- ln1_gain_grad: float32 [2048], P(('seq', 'fsdp'))
- ln1_bias_grad: float32 [2048], P(('seq', 'fsdp'))
- w_qkv_grad: float32 [2048, 6144], P(('seq', 'fsdp'))
- qkv_bias_grad: float32 [6144], P(('seq', 'fsdp'))
- w_out_grad: float32 [2048, 2048], P(('seq', 'fsdp'))
- ln2_gain_grad: float32 [2048], P(('seq', 'fsdp'))
- ln2_bias_grad: float32 [2048], P(('seq', 'fsdp'))
- w_gate_grad: float32 [2048, 5632], P(('seq', 'fsdp'))
- w_up_grad: float32 [2048, 5632], P(('seq', 'fsdp'))
- w_down_grad: float32 [2048, 5632], P(('seq', 'fsdp'))
Inputs may be any that keep to these rules, and one draw needn't show every extreme that they name: `seq_lengths`: each group holds two sequences, in this order, each padded to whole 128-token blocks; together their blocks fill the group's 8 blocks, and each has less than half a block of padding. `slot_block`: each row is an order of the group's block numbers; slot s lies on seq device s.
All inputs are finite; a program needn't handle non-finite values.
Results may differ from a plain program's by a relative error of at most 0.018.
Values may be sent and summed in bfloat16 or wider, within the bound.
A program may use at most 704 MiB of HBM per device.

v0:
```python
import jax
import jax.numpy as jnp
from jax import lax
from jax.sharding import PartitionSpec as P

D = 2048
HEADS = 32
HEAD_DIM = 64
ROT = 16
FF = 5632
BLOCK = 128


EPS = 1e-05
NEG = -1e30


def token_places(lengths, slot_table):
    first_pad = (lengths[0] + BLOCK - 1) // BLOCK * BLOCK
    offsets = jnp.arange(BLOCK, dtype=jnp.int32)
    placed = (slot_table[:, None] * BLOCK + offsets[None, :]).reshape(-1)
    second = (placed >= first_pad).astype(jnp.int32)
    position = placed - second * first_pad
    length_limit = jnp.where(second == 1, lengths[1], lengths[0])
    return (second, position, position < length_limit)


def rotary_tables(position):
    freq_steps = jnp.arange(ROT // 2, dtype=jnp.float32)
    inverse = 10000.0 ** (-2.0 * freq_steps / ROT)
    phases = position.astype(jnp.float32)[:, None] * inverse[None, :]
    return (jnp.cos(phases), jnp.sin(phases))


def rotate(values, cosine, sines, direction):
    shaped = values.reshape(values.shape[0], HEADS, HEAD_DIM)
    half_rot = ROT // 2
    front = shaped[..., :half_rot]
    behind = shaped[..., half_rot:ROT]
    cos_part = cosine[:, None, :]
    sin_part = sines[:, None, :] * direction
    turned = jnp.concatenate(
        [
            front * cos_part - behind * sin_part,
            behind * cos_part + front * sin_part,
            shaped[..., ROT:],
        ],
        axis=-1,
    )
    return turned.reshape(values.shape)


def layer_norm(values, gain, bias):
    average = jnp.mean(values, axis=-1, keepdims=True)
    centred = values - average
    inv_scale = lax.rsqrt(jnp.mean(centred * centred, axis=-1, keepdims=True) + EPS)
    normed = centred * inv_scale
    return (normed, inv_scale, normed * gain + bias)


def norm_back(grad_in, normed, inv_scale, gain):
    scaled = grad_in * gain
    return inv_scale * (
        scaled
        - jnp.mean(scaled, axis=-1, keepdims=True)
        - normed * jnp.mean(scaled * normed, axis=-1, keepdims=True)
    )


def contract_tokens(left, right):
    return lax.dot_general(
        left, right, (((0,), (0,)), ((), ())), preferred_element_type=jnp.float32
    )


def contract_width(left, right):
    return lax.dot_general(
        left, right, (((1,), (1,)), ((), ())), preferred_element_type=jnp.float32
    )


def attention_scores(query_heads, key_heads, allowed):
    raw = jnp.einsum(
        "thd,shd->hts", query_heads, key_heads, preferred_element_type=jnp.float32
    ) * HEAD_DIM ** (-0.5)
    return jnp.where(allowed[None], raw, NEG)


def attention_rows(lowered_one, joined_grad, attended, branch_grad):
    return jnp.concatenate(
        [contract_tokens(lowered_one, joined_grad), contract_tokens(attended, branch_grad)], axis=1
    )


def mlp_rows(lowered_two, gate_grad, up_grad, grad_out, inner):
    return jnp.concatenate(
        [
            contract_tokens(lowered_two, gate_grad),
            contract_tokens(lowered_two, up_grad),
            contract_tokens(grad_out, inner),
        ],
        axis=1,
    )


def body(
    hidden_in,
    cotangent,
    seq_lengths,
    slot_block,
    ln1_gain,
    ln1_bias,
    w_qkv,
    qkv_bias,
    w_out,
    ln2_gain,
    ln2_bias,
    w_gate,
    w_up,
    w_down,
):
    token_count = hidden_in.shape[1]
    score_scale = HEAD_DIM ** (-0.5)
    second, position, valid = token_places(seq_lengths[0], slot_block[0])
    anchor = lax.axis_index("seq") * token_count
    local_second = lax.dynamic_slice_in_dim(second, anchor, token_count, 0)
    local_position = lax.dynamic_slice_in_dim(position, anchor, token_count, 0)
    local_valid = lax.dynamic_slice_in_dim(valid, anchor, token_count, 0)
    allowed = (
        (local_second[:, None] == second[None, :])
        & (position[None, :] <= local_position[:, None])
        & valid[None, :]
    )
    cosine, sines = rotary_tables(local_position)
    hidden = hidden_in[0].astype(jnp.float32)
    attention_full = (
        lax.all_gather(ln1_gain, ("seq", "fsdp"), axis=0, tiled=True),
        lax.all_gather(ln1_bias, ("seq", "fsdp"), axis=0, tiled=True),
        lax.all_gather(w_qkv, ("seq", "fsdp"), axis=0, tiled=True),
        lax.all_gather(qkv_bias, ("seq", "fsdp"), axis=0, tiled=True),
        lax.all_gather(w_out, ("seq", "fsdp"), axis=0, tiled=True),
    )
    gain_one, bias_one, qkv_full, shift_full, out_full = attention_full
    normed_one, inv_one, shifted_one = layer_norm(
        hidden, gain_one.astype(jnp.float32), bias_one.astype(jnp.float32)
    )
    lowered_one = shifted_one.astype(jnp.bfloat16)
    joined = jnp.dot(lowered_one, qkv_full, preferred_element_type=jnp.float32) + shift_full.astype(
        jnp.float32
    )
    queries = rotate(joined[:, :D], cosine, sines, 1.0).astype(jnp.bfloat16)
    own_keys = rotate(joined[:, D : 2 * D], cosine, sines, 1.0).astype(jnp.bfloat16)
    own_values = joined[:, 2 * D :].astype(jnp.bfloat16)
    key_rows, value_rows = (
        lax.all_gather(own_keys, "seq", axis=0, tiled=True),
        lax.all_gather(own_values, "seq", axis=0, tiled=True),
    )
    query_heads = queries.reshape(token_count, HEADS, HEAD_DIM)
    key_heads = key_rows.reshape(-1, HEADS, HEAD_DIM)
    value_heads = value_rows.reshape(-1, HEADS, HEAD_DIM)
    scores = attention_scores(query_heads, key_heads, allowed)
    highest = jnp.max(scores, axis=-1, keepdims=True)
    log_total = highest + jnp.log(jnp.sum(jnp.exp(scores - highest), axis=-1, keepdims=True))
    weights = jnp.exp(scores - log_total).astype(jnp.bfloat16)
    mixed = jnp.einsum("hts,shd->thd", weights, value_heads, preferred_element_type=jnp.float32)
    attended = mixed.reshape(token_count, D).astype(jnp.bfloat16)
    middle = hidden + jnp.dot(attended, out_full, preferred_element_type=jnp.float32)
    mlp_full = (
        lax.all_gather(ln2_gain, ("seq", "fsdp"), axis=0, tiled=True),
        lax.all_gather(ln2_bias, ("seq", "fsdp"), axis=0, tiled=True),
        lax.all_gather(w_gate, ("seq", "fsdp"), axis=0, tiled=True),
        lax.all_gather(w_up, ("seq", "fsdp"), axis=0, tiled=True),
        lax.all_gather(w_down, ("seq", "fsdp"), axis=0, tiled=True),
    )
    gain_two, bias_two, gate_full, up_full, down_full = mlp_full
    normed_two, inv_two, shifted_two = layer_norm(
        middle, gain_two.astype(jnp.float32), bias_two.astype(jnp.float32)
    )
    lowered_two = shifted_two.astype(jnp.bfloat16)
    gate = jnp.dot(lowered_two, gate_full, preferred_element_type=jnp.float32)
    up_proj = jnp.dot(lowered_two, up_full, preferred_element_type=jnp.float32)
    activated = jax.nn.silu(gate)
    inner = (activated * up_proj).astype(jnp.bfloat16)
    hidden_out = (middle + contract_width(inner, down_full)).astype(jnp.bfloat16)
    back_mlp = (
        lax.all_gather(ln2_gain, ("seq", "fsdp"), axis=0, tiled=True),
        lax.all_gather(ln2_bias, ("seq", "fsdp"), axis=0, tiled=True),
        lax.all_gather(w_gate, ("seq", "fsdp"), axis=0, tiled=True),
        lax.all_gather(w_up, ("seq", "fsdp"), axis=0, tiled=True),
        lax.all_gather(w_down, ("seq", "fsdp"), axis=0, tiled=True),
    )
    back_attention = (
        lax.all_gather(ln1_gain, ("seq", "fsdp"), axis=0, tiled=True),
        lax.all_gather(ln1_bias, ("seq", "fsdp"), axis=0, tiled=True),
        lax.all_gather(w_qkv, ("seq", "fsdp"), axis=0, tiled=True),
        lax.all_gather(qkv_bias, ("seq", "fsdp"), axis=0, tiled=True),
        lax.all_gather(w_out, ("seq", "fsdp"), axis=0, tiled=True),
    )
    gain_two_back, unused_two, gate_back, up_back, down_back = back_mlp
    gain_one_back, unused_one, qkv_back, unused_shift, out_back = back_attention
    grad_out = cotangent[0] * local_valid[:, None].astype(jnp.bfloat16)
    inner_grad = jnp.dot(grad_out, down_back, preferred_element_type=jnp.float32)
    sigmoid_gate = jax.nn.sigmoid(gate)
    gate_grad = (inner_grad * up_proj * sigmoid_gate * (1.0 + gate * (1.0 - sigmoid_gate))).astype(
        jnp.bfloat16
    )
    up_grad = (inner_grad * activated).astype(jnp.bfloat16)
    normed_two_grad = contract_width(gate_grad, gate_back) + contract_width(up_grad, up_back)
    middle_grad = grad_out.astype(jnp.float32) + norm_back(
        normed_two_grad, normed_two, inv_two, gain_two_back.astype(jnp.float32)
    )
    branch_grad = middle_grad.astype(jnp.bfloat16)
    attended_grad = contract_width(branch_grad, out_back).astype(jnp.bfloat16)
    grad_heads = attended_grad.reshape(token_count, HEADS, HEAD_DIM)
    again_scores = attention_scores(query_heads, key_heads, allowed)
    prob_rows = jnp.exp(again_scores - log_total)
    prob_grad = jnp.einsum(
        "thd,shd->hts", grad_heads, value_heads, preferred_element_type=jnp.float32
    )
    score_grad = (
        prob_rows * (prob_grad - jnp.sum(prob_rows * prob_grad, axis=-1, keepdims=True))
    ).astype(jnp.bfloat16)
    query_grad = (
        jnp.einsum("hts,shd->thd", score_grad, key_heads, preferred_element_type=jnp.float32)
        * score_scale
    )
    key_part = (
        jnp.einsum("hts,thd->shd", score_grad, query_heads, preferred_element_type=jnp.float32)
        * score_scale
    )
    value_part = jnp.einsum(
        "hts,thd->shd",
        prob_rows.astype(jnp.bfloat16),
        grad_heads,
        preferred_element_type=jnp.float32,
    )
    key_grad, value_grad = (
        lax.psum_scatter(
            key_part.reshape(-1, D).astype(jnp.bfloat16), "seq", scatter_dimension=0, tiled=True
        ).astype(jnp.float32),
        lax.psum_scatter(
            value_part.reshape(-1, D).astype(jnp.bfloat16), "seq", scatter_dimension=0, tiled=True
        ).astype(jnp.float32),
    )
    joined_grad = jnp.concatenate(
        [
            rotate(query_grad.reshape(token_count, D), cosine, sines, -1.0),
            rotate(key_grad, cosine, sines, -1.0),
            value_grad,
        ],
        axis=1,
    ).astype(jnp.bfloat16)
    normed_one_grad = contract_width(joined_grad, qkv_back)
    input_grad = middle_grad + norm_back(
        normed_one_grad, normed_one, inv_one, gain_one_back.astype(jnp.float32)
    )
    attention_sums = lax.psum_scatter(
        attention_rows(lowered_one, joined_grad, attended, branch_grad),
        ("seq", "fsdp"),
        scatter_dimension=0,
        tiled=True,
    )
    mlp_sums = lax.psum_scatter(
        mlp_rows(lowered_two, gate_grad, up_grad, grad_out, inner),
        ("seq", "fsdp"),
        scatter_dimension=0,
        tiled=True,
    )
    small_terms = (
        jnp.sum(normed_one_grad * normed_one, axis=0),
        jnp.sum(normed_one_grad, axis=0),
        jnp.sum(joined_grad.astype(jnp.float32), axis=0),
        jnp.sum(normed_two_grad * normed_two, axis=0),
        jnp.sum(normed_two_grad, axis=0),
    )
    gain_one_grad, bias_one_grad, shift_grad, gain_two_grad, bias_two_grad = (
        lax.psum_scatter(small_terms[0], ("seq", "fsdp"), scatter_dimension=0, tiled=True),
        lax.psum_scatter(small_terms[1], ("seq", "fsdp"), scatter_dimension=0, tiled=True),
        lax.psum_scatter(small_terms[2], ("seq", "fsdp"), scatter_dimension=0, tiled=True),
        lax.psum_scatter(small_terms[3], ("seq", "fsdp"), scatter_dimension=0, tiled=True),
        lax.psum_scatter(small_terms[4], ("seq", "fsdp"), scatter_dimension=0, tiled=True),
    )
    return (
        hidden_out[None],
        input_grad[None],
        gain_one_grad,
        bias_one_grad,
        attention_sums[:, : 3 * D],
        shift_grad,
        attention_sums[:, 3 * D :],
        gain_two_grad,
        bias_two_grad,
        mlp_sums[:, :FF],
        mlp_sums[:, FF : 2 * FF],
        mlp_sums[:, 2 * FF :],
    )


def solution(mesh):
    placed = (
        P("fsdp", "seq", None),
        P("fsdp", "seq", None),
        P("fsdp", None),
        P("fsdp", None),
        P(("seq", "fsdp")),
        P(("seq", "fsdp")),
        P(("seq", "fsdp"), None),
        P(("seq", "fsdp")),
        P(("seq", "fsdp"), None),
        P(("seq", "fsdp")),
        P(("seq", "fsdp")),
        P(("seq", "fsdp"), None),
        P(("seq", "fsdp"), None),
        P(("seq", "fsdp"), None),
    )
    return jax.shard_map(
        body,
        mesh=mesh,
        in_specs=placed,
        out_specs=(
            P("fsdp", "seq", None),
            P("fsdp", "seq", None),
            P(("seq", "fsdp")),
            P(("seq", "fsdp")),
            P(("seq", "fsdp"), None),
            P(("seq", "fsdp")),
            P(("seq", "fsdp"), None),
            P(("seq", "fsdp")),
            P(("seq", "fsdp")),
            P(("seq", "fsdp"), None),
            P(("seq", "fsdp"), None),
            P(("seq", "fsdp"), None),
        ),
        check_vma=False,
    )
```

profile of v0, /device:TPU:1, one launch (start us, length us, event | category | flops | bytes accessed | tf_op | source)
XLA Modules:
  0.0 3846.8 jit_solution(4942496717065947758)
XLA Ops:
  12.2 69.4 %all-reduce.11 = (bf16[6144]{0:T(1024)(128)(2,1)S(1)}, bf16[2048]{0:T(1024)(128)(2,1)S(1)}, bf16[2048]{0:T(1024)(128)(2,1)S(1)}, bf16[2048]{0:T(1024)(128)(2,1)S(1)}, bf16[2048]{0:T(1024)(128)(2,1)S(1)}) all-reduce(bf16[6144]{0:T(1024)(128)(2,1)S(1)} %dynamic-update-slice.2, ...), channel_id=1, replica_groups=mesh['seq'=8,'fsdp'=16] {'seq','fsdp'}, use_global_device_ids=true, to_apply=%add.2 | all-reduce | flops 14336 | bytes 57344
  84.2 156.4 %all-gather.8.cloned.1.call-done = bf16[2048,6144]{1,0:T(8,128)(2,1)} async-done(((bf16[16,6144]{1,0:T(8,128)(2,1)}), bf16[2048,6144]{1,0:T(8,128)(2,1)}) %all-gather.8.cloned.1.call-update) | async-done | bytes 25165840 | tf_op jit(solution)/shard_map/all_gather | solution.py:139
  240.6 10.3 convolution_add_fusion
  264.5 57.5 %all-gather.10.cloned.1.call-done = bf16[1024,2048]{1,0:T(8,128)(2,1)} async-done(((bf16[128,2048]{1,0:T(8,128)(2,1)}), bf16[1024,2048]{1,0:T(8,128)(2,1)}) %all-gather.10.cloned.1.call-update) | async-done | bytes 4194320 | tf_op jit(solution)/shard_map/all_gather | solution.py:156
  328.4 71.9 %all-gather.12.cloned.1.call-done = bf16[1024,2048]{0,1:T(8,128)(2,1)} async-done(((bf16[128,2048]{0,1:T(8,128)(2,1)}), bf16[1024,2048]{0,1:T(8,128)(2,1)}) %all-gather.12.cloned.1.call-update) | async-done | bytes 4194320 | tf_op jit(solution)/shard_map/all_gather | solution.py:155
  412.4 8.4 convolution_convert_fusion.2
  420.8 183.4 %all-gather.14.cloned.1.call-done = bf16[2048,2048]{1,0:T(8,128)(2,1)} async-done(((bf16[16,2048]{1,0:T(8,128)(2,1)}), bf16[2048,2048]{1,0:T(8,128)(2,1)}) %all-gather.14.cloned.1.call-update) | async-done | bytes 8388624 | tf_op jit(solution)/shard_map/all_gather | solution.py:141
  609.5 219.8 %all-gather.16.cloned.1.call-done = bf16[2048,5632]{1,0:T(8,128)(2,1)} async-done(((bf16[16,5632]{1,0:T(8,128)(2,1)}), bf16[2048,5632]{1,0:T(8,128)(2,1)}) %all-gather.16.cloned.1.call-update) | async-done | bytes 23068688 | tf_op jit(solution)/shard_map/all_gather | solution.py:171
  829.4 12.3 fusion.48
  841.7 212.2 %all-gather.18.cloned.1.call-done = bf16[2048,5632]{1,0:T(8,128)(2,1)} async-done(((bf16[16,5632]{1,0:T(8,128)(2,1)}), bf16[2048,5632]{1,0:T(8,128)(2,1)}) %all-gather.18.cloned.1.call-update) | async-done | bytes 23068688 | tf_op jit(solution)/shard_map/all_gather | solution.py:172
  1053.9 12.3 fusion.49
  1066.2 213.0 %all-gather.20.cloned.1.call-done = bf16[2048,5632]{1,0:T(8,128)(2,1)} async-done(((bf16[16,5632]{1,0:T(8,128)(2,1)}), bf16[2048,5632]{1,0:T(8,128)(2,1)}) %all-gather.20.cloned.1.call-update) | async-done | bytes 23068688 | tf_op jit(solution)/shard_map/all_gather | solution.py:173
  1279.3 14.5 multiply_convert_fusion.2
  1293.8 12.8 fusion.50
  1306.7 13.9 multiply_reduce_fusion.1
  1331.2 16.3 multiply_reduce_fusion
  1347.5 12.0 multiply_convert_fusion
  1370.9 9.5 convolution_convert_fusion
  1395.8 8.1 fusion.24
  1403.9 49.6 %reduce-scatter.13.cloned.1.call-done = bf16[128,2048]{1,0:T(8,128)(2,1)} async-done(((bf16[1024,2048]{1,0:T(8,128)(2,1)}), bf16[128,2048]{1,0:T(8,128)(2,1)}) %reduce-scatter.13.cloned.1.call-update) | async-done | bytes 524304
  1456.2 84.6 %reduce-scatter.15.cloned.1.call-done = bf16[128,2048]{1,0:T(8,128)(2,1)} async-done(((bf16[1024,2048]{1,0:T(8,128)(2,1)}), bf16[128,2048]{1,0:T(8,128)(2,1)}) %reduce-scatter.15.cloned.1.call-update) | async-done | bytes 524304
  1542.2 21.5 fusion.39
  1563.7 43.5 %pad_maximum_fusion.1 = f32[2048,8192]{1,0:T(8,128)} fusion(f32[2048,2048]{1,0:T(8,128)} %fusion.24, f32[2048,6144]{1,0:T(8,128)} %fusion.39), kind=kLoop, calls=%fused_computation.1 | loop fusion | flops 16777216 | bytes 134217728 | tf_op jit(solution)/shard_map/concatenate | solution.py:90
  1608.7 18.8 fusion.52
  1627.5 18.4 fusion.51
  1645.9 18.5 fusion.22
  1664.4 89.6 %pad_maximum_fusion = f32[2048,16896]{1,0:T(8,128)} fusion(f32[2048,5632]{1,0:T(8,128)} %fusion.22, f32[2048,5632]{1,0:T(8,128)} %fusion.52, f32[2048,5632]{1,0:T(8,128)} %fusion.51), kind=kLoop, calls=%fused_computation | loop fusion | flops 69206016 | bytes 276824064 | tf_op jit(solution)/shard_map/concatenate | solution.py:96
  1755.2 13.3 fusion.4
  1769.1 14.0 fusion.20
  1783.2 70.2 %all-reduce.10 = (f32[2048]{0:T(1024)S(1)}, f32[2048]{0:T(1024)S(1)}, f32[6144]{0:T(1024)S(1)}, f32[2048]{0:T(1024)S(1)}, f32[2048]{0:T(1024)S(1)}) all-reduce(f32[2048]{0:T(1024)S(1)} %get-tuple-element.14, f32[2048]{0:T(1024)S(1)} %get-tuple-element.19, ...), channel_id=4, replica_groups=mesh['seq'=8,'fsdp'=16] {'seq','fsdp'}, use_global_device_ids=true, to_apply=%region_14.15.clone | all-reduce | flops 14336 | bytes 114688
  1857.7 494.8 %reduce-scatter.9.cloned.1.call-done = f32[16,8192]{1,0:T(8,128)} async-done(((f32[2048,8192]{1,0:T(8,128)}), f32[16,8192]{1,0:T(8,128)}) %reduce-scatter.9.cloned.1.call-update) | async-done | bytes 524304 | tf_op jit(solution)/shard_map/reduce_scatter | solution.py:257
  2355.9 1481.8 %reduce-scatter.11.cloned.1.call-done = f32[16,16896]{1,0:T(8,128)} async-done(((f32[2048,16896]{1,0:T(8,128)}), f32[16,16896]{1,0:T(8,128)}) %reduce-scatter.11.cloned.1.call-update) | async-done | bytes 1081360 | tf_op jit(solution)/shard_map/reduce_scatter | solution.py:263
  (200 shorter events, 98.4 us)
Async XLA Ops:
  7.2 233.4 %all-gather.8.cloned.1.call-start = ((), (), s32[]{:S(2)}) async-start(), calls=%async_computation.4 | async-start | bytes 25362432 | tf_op jit(solution)/shard_map/all_gather | solution.py:139
  7.9 314.1 %all-gather.10.cloned.1.call-start = ((), (), s32[]{:S(2)}) async-start(), calls=%async_computation.5 | async-start | bytes 4718592 | tf_op jit(solution)/shard_map/all_gather | solution.py:156
  81.6 1460.5 %copy-start.31 = (f32[2048]{0:T(1024)}, f32[2048]{0:T(1024)S(1)}, u32[]{:S(2)}) copy-start(f32[2048]{0:T(1024)S(1)} %convert_element_type.116) | copy-start | bytes 24580
  82.8 168.1 %copy-start.38 = (f32[128]{0:T(128)}, f32[128]{0:T(128)S(1)}, u32[]{:S(2)}) copy-start(f32[128]{0:T(128)S(1)} %broadcast_multiply_fusion.6) | copy-start | bytes 1540
  84.2 166.7 %copy-start.42 = (f32[128]{0:T(128)}, f32[128]{0:T(128)S(1)}, u32[]{:S(2)}) copy-start(f32[128]{0:T(128)S(1)} %add_rsqrt_fusion.1) | copy-start | bytes 1540
  84.2 167.6 %copy-start.50 = (s32[1,2]{1,0:T(1,128)S(1)}, s32[1,2]{1,0:T(1,128)}, u32[]{:S(2)}) copy-start(s32[1,2]{1,0:T(1,128)} %param.16) | copy-start | bytes 28
  84.2 168.9 %copy-start.51 = (s32[1,8]{1,0:T(1,128)S(1)}, s32[1,8]{1,0:T(1,128)}, u32[]{:S(2)}) copy-start(s32[1,8]{1,0:T(1,128)} %param.17) | copy-start | bytes 100
  251.8 148.6 %all-gather.12.cloned.1.call-start = ((), (), s32[]{:S(2)}) async-start(), calls=%async_computation.6 | async-start | bytes 4718592 | tf_op jit(solution)/shard_map/all_gather | solution.py:155
  258.8 146.4 %copy-start.27 = (bf16[128,32,8]{0,2,1:T(8,128)(2,1)}, bf16[128,32,8]{0,2,1:T(8,128)(2,1)S(1)}, u32[]{:S(2)}) copy-start(bf16[128,32,8]{0,2,1:T(8,128)(2,1)S(1)} %get-tuple-element.44) | copy-start | bytes 196612
  258.8 146.4 %copy-start.29 = (bf16[128,32,8]{0,2,1:T(8,128)(2,1)}, bf16[128,32,8]{0,2,1:T(8,128)(2,1)S(1)}, u32[]{:S(2)}) copy-start(bf16[128,32,8]{0,2,1:T(8,128)(2,1)S(1)} %get-tuple-element.45) | copy-start | bytes 196612
  259.7 344.6 %all-gather.14.cloned.1.call-start = ((), (), s32[]{:S(2)}) async-start(), calls=%async_computation.7 | async-start | bytes 8454144 | tf_op jit(solution)/shard_map/all_gather | solution.py:141
  260.2 569.1 %all-gather.16.cloned.1.call-start = ((), (), s32[]{:S(2)}) async-start(), calls=%async_computation.8 | async-start | bytes 23248896 | tf_op jit(solution)/shard_map/all_gather | solution.py:171
  260.8 793.1 %all-gather.18.cloned.1.call-start = ((), (), s32[]{:S(2)}) async-start(), calls=%async_computation.9 | async-start | bytes 23248896 | tf_op jit(solution)/shard_map/all_gather | solution.py:172
  261.4 1017.8 %all-gather.20.cloned.1.call-start = ((), (), s32[]{:S(2)}) async-start(), calls=%async_computation.10 | async-start | bytes 23248896 | tf_op jit(solution)/shard_map/all_gather | solution.py:173
  262.2 1191.4 %reduce-scatter.13.cloned.1.call-start = ((), (), s32[]{:S(2)}) async-start(), calls=%async_computation.13 | async-start | bytes 4718592
  263.7 345.6 %copy-start.35 = (f32[2048]{0:T(1024)}, f32[2048]{0:T(1024)S(1)}, u32[]{:S(2)}) copy-start(f32[2048]{0:T(1024)S(1)} %convert_element_type.127) | copy-start | bytes 24580
  264.4 147.9 %copy-start.22 = (pred[128,1024]{1,0:T(8,128)(4,1)}, pred[128,1024]{1,0:T(8,128)(4,1)S(1)}, u32[]{:S(2)}) copy-start(pred[128,1024]{1,0:T(8,128)(4,1)S(1)} %and_and_fusion) | copy-start | bytes 393220
  412.4 191.9 %copy-start.4 = (bf16[1,128,2048]{2,1,0:T(8,128)(2,1)S(1)}, bf16[1,128,2048]{2,1,0:T(8,128)(2,1)}, u32[]{:S(2)}) copy-start(bf16[1,128,2048]{2,1,0:T(8,128)(2,1)} %param.14) | copy-start | bytes 1572868
  609.0 711.6 %copy-start.2 = (f32[128,2048]{1,0:T(8,128)}, f32[128,2048]{1,0:T(8,128)S(1)}, u32[]{:S(2)}) copy-start(f32[128,2048]{1,0:T(8,128)S(1)} %get-tuple-element.62) | copy-start | bytes 3145732
  609.0 220.4 %copy-start.44 = (f32[128]{0:T(128)}, f32[128]{0:T(128)S(1)}, u32[]{:S(2)}) copy-start(f32[128]{0:T(128)S(1)} %broadcast_multiply_fusion.5) | copy-start | bytes 1540
  609.3 220.1 %copy-start.48 = (f32[128]{0:T(128)}, f32[128]{0:T(128)S(1)}, u32[]{:S(2)}) copy-start(f32[128]{0:T(128)S(1)} %add_rsqrt_fusion) | copy-start | bytes 1540
  609.5 444.4 %copy-start.9 = (bf16[128,2048]{1,0:T(8,128)(2,1)}, bf16[128,2048]{1,0:T(8,128)(2,1)S(1)}, u32[]{:S(2)}) copy-start(bf16[128,2048]{1,0:T(8,128)(2,1)S(1)} %add_convert_fusion) | copy-start | bytes 1572868
  841.7 437.5 %copy-start.25 = (bf16[1,128,2048]{2,1,0:T(8,128)(2,1)S(1)}, bf16[1,128,2048]{2,1,0:T(8,128)(2,1)}, u32[]{:S(2)}) copy-start(bf16[1,128,2048]{2,1,0:T(8,128)(2,1)} %param.15) | copy-start | bytes 1572868
  1322.4 73.4 %copy-start.6 = (f32[128,2048]{1,0:T(8,128)}, f32[128,2048]{1,0:T(8,128)S(1)}, u32[]{:S(2)}) copy-start(f32[128,2048]{1,0:T(8,128)S(1)} %multiply_add_fusion) | copy-start | bytes 3145732
  1370.8 170.0 %reduce-scatter.15.cloned.1.call-start = ((), (), s32[]{:S(2)}) async-start(), calls=%async_computation.14 | async-start | bytes 4718592
  1386.9 965.7 %reduce-scatter.9.cloned.1.call-start = ((), (), s32[]{:S(2)}) async-start(), calls=%async_computation.11 | async-start | bytes 67633152 | tf_op jit(solution)/shard_map/reduce_scatter | solution.py:257
  1456.2 107.5 %copy-start.16 = (bf16[128,32,64]{0,2,1:T(8,128)(2,1)}, bf16[128,32,64]{0,2,1:T(8,128)(2,1)S(1)}, u32[]{:S(2)}) copy-start(bf16[128,32,64]{0,2,1:T(8,128)(2,1)S(1)} %pad_maximum_fusion.6) | copy-start | bytes 1572868
  1456.2 107.5 %copy-start.18 = (bf16[128,32,64]{0,2,1:T(8,128)(2,1)}, bf16[128,32,64]{0,2,1:T(8,128)(2,1)S(1)}, u32[]{:S(2)}) copy-start(bf16[128,32,64]{0,2,1:T(8,128)(2,1)S(1)} %pad_maximum_fusion.5) | copy-start | bytes 1572868
  1542.2 21.6 copy-start.20
  1607.2 20.3 copy-start.12
  1607.2 2230.5 %reduce-scatter.11.cloned.1.call-start = ((), (), s32[]{:S(2)}) async-start(), calls=%async_computation.12 | async-start | bytes 139493376 | tf_op jit(solution)/shard_map/reduce_scatter | solution.py:263
  1769.1 87.2 %copy-start.7 = (f32[128,2048]{1,0:T(8,128)S(1)}, f32[128,2048]{1,0:T(8,128)}, u32[]{:S(2)}) copy-start(f32[128,2048]{1,0:T(8,128)} %copy-done.6) | copy-start | bytes 3145732
  (31 other events, 356.2 us)
Sparse Core Ops, SparseCore 0:
  9.7 230.8 all-gather.7
  251.9 70.0 all-gather.9
  324.8 75.5 all-gather.11
  401.9 202.2 all-gather.13
  605.8 223.5 all-gather.15
  830.9 222.9 all-gather.17
  1055.6 223.5 all-gather.19
  1370.9 82.5 reduce-scatter.12
  1457.4 83.3 reduce-scatter.14
  1607.3 745.2 reduce-scatter.8
  2355.0 1482.6 reduce-scatter.10
where the time goes:
time: 3860 us; the launch traced here: 3850 us
  waiting for transfers between devices  3230 us (84%)
  matrix products  251 us (7%)
  other arithmetic  161 us (4%)
  blocking collectives  140 us (4%)
  local copies, waits for them, and re-layouts  49.9 us (1%)
    reduce_scatter x1, waiting for transfers between devices, body(): lax.psum_scatter(mlp_rows(lowered_two, gate_grad, up_grad, grad_out, inne...  1480 us
    reduce_scatter x1, waiting for transfers between devices, body(): lax.psum_scatter(attention_rows(lowered_one, joined_grad, attended, branc...  495 us
    all_gather x1, waiting for transfers between devices, body(): lax.all_gather(w_gate, ('seq', 'fsdp'), axis=0, tiled=True)  220 us
    all_gather x1, waiting for transfers between devices, body(): lax.all_gather(w_down, ('seq', 'fsdp'), axis=0, tiled=True)  213 us
    all_gather x1, waiting for transfers between devices, body(): lax.all_gather(w_up, ('seq', 'fsdp'), axis=0, tiled=True)  212 us
    all_gather x1, waiting for transfers between devices, body(): lax.all_gather(w_out, ('seq', 'fsdp'), axis=0, tiled=True)  183 us
    all_gather x1, waiting for transfers between devices, body(): lax.all_gather(w_qkv, ('seq', 'fsdp'), axis=0, tiled=True)  156 us
    unnamed x2, blocking collectives  140 us
  transfers between devices with their start and end apart: 11, of which 11 were waited for; matrix products, arithmetic and copies ran while one was open for 7% of the time, Pallas kernels for 0%

commit v1 on v0

v1 whole, which is shorter than its diff:
```python
import jax
import jax.numpy as jnp
from jax import lax
from jax.sharding import Mesh
from jax.sharding import PartitionSpec as P

D = 2048
HEADS = 32
HEAD_DIM = 64
ROT = 16
FF = 5632
BLOCK = 128
TP = 8
HD = D // TP
FC = FF // TP

EPS = 1e-05
NEG = -1e30
SCALE = HEAD_DIM ** (-0.5)
TPA = ("y", "core")
TOK = ("core", "y")
XZ = ("x", "zh", "zl")
ROWS = ("zh", "y", "x", "zl", "core")
GRP = ("x", "zl", "core")
SLOT = ("zh", "y")


def permute_features(v):
    lead = v.shape[:-1]
    n = len(lead)
    v = v.reshape(lead + (2, 4, 4, 2, 32))
    v = v.transpose(tuple(range(n)) + (n + 2, n, n + 3, n + 1, n + 4))
    return v.reshape(lead + (D,))


def restore_features(v):
    lead = v.shape[:-1]
    n = len(lead)
    v = v.reshape(lead + (4, 2, 2, 4, 32))
    v = v.transpose(tuple(range(n)) + (n + 1, n + 3, n, n + 2, n + 4))
    return v.reshape(lead + (D,))


def block_places(lengths, blocks):
    first_pad = (lengths[0] + BLOCK - 1) // BLOCK * BLOCK
    offsets = jnp.arange(BLOCK, dtype=jnp.int32)
    placed = (blocks[:, None] * BLOCK + offsets[None, :]).reshape(-1)
    second = (placed >= first_pad).astype(jnp.int32)
    position = placed - second * first_pad
    limit = jnp.where(second == 1, lengths[1], lengths[0])
    return second, position, position < limit


def rotary_tables(position):
    freq_steps = jnp.arange(ROT // 2, dtype=jnp.float32)
    inverse = 10000.0 ** (-2.0 * freq_steps / ROT)
    phases = position.astype(jnp.float32)[..., None] * inverse
    return jnp.cos(phases), jnp.sin(phases)


def rotate(shaped, cosine, sines, direction):
    half = ROT // 2
    front = shaped[..., :half]
    behind = shaped[..., half:ROT]
    c = cosine[:, :, None, :]
    s = sines[:, :, None, :] * direction
    return jnp.concatenate(
        [front * c - behind * s, behind * c + front * s, shaped[..., ROT:]], axis=-1
    )


def layer_norm(values):
    average = jnp.mean(values, axis=-1, keepdims=True)
    centred = values - average
    inv_scale = lax.rsqrt(jnp.mean(centred * centred, axis=-1, keepdims=True) + EPS)
    return centred * inv_scale, inv_scale


def norm_back(grad_in, normed, inv_scale, gain):
    scaled = grad_in * gain
    return inv_scale * (
        scaled
        - jnp.mean(scaled, axis=-1, keepdims=True)
        - normed * jnp.mean(scaled * normed, axis=-1, keepdims=True)
    )


def mm(a, b):
    return jnp.dot(a, b, preferred_element_type=jnp.float32)


def mm_nt(a, b):
    return lax.dot_general(a, b, (((1,), (1,)), ((), ())), preferred_element_type=jnp.float32)


def mm_tn(a, b):
    return lax.dot_general(a, b, (((0,), (0,)), ((), ())), preferred_element_type=jnp.float32)


def gather_weight(w):
    w = lax.all_to_all(w, TPA, 0, 0, tiled=True).reshape(BLOCK, -1)
    return lax.all_gather(w, XZ, axis=0, tiled=True)


def scatter_grad(g):
    g = lax.psum_scatter(g.astype(jnp.bfloat16), XZ, scatter_dimension=0, tiled=True)
    return lax.all_to_all(g.reshape(TP, 16, -1), TPA, 0, 0, tiled=True)


def gather_tokens(v):
    return lax.all_gather(v, TOK, axis=0, tiled=True)


def scatter_tokens(v):
    return lax.psum_scatter(v, TOK, scatter_dimension=0, tiled=True)


def body(
    hidden_in,
    cotangent,
    seq_lengths,
    slot_block,
    ln1_gain,
    ln1_bias,
    w_qkv,
    qkv_bias,
    w_out,
    ln2_gain,
    ln2_bias,
    w_gate,
    w_up,
    w_down,
):
    bf = jnp.bfloat16
    f32 = jnp.float32
    zh = lax.axis_index("zh")
    y = lax.axis_index("y")
    core = lax.axis_index("core")

    part_qkv = w_qkv.reshape(16, 3, 2, 4, HD).transpose(3, 2, 0, 1, 4).reshape(TP, 16, 3 * HD)
    part_gate, part_up, part_down = (
        w.reshape(16, TP, FC).transpose(1, 0, 2) for w in (w_gate, w_up, w_down)
    )
    qkv_full = gather_weight(part_qkv)
    out_rows = lax.all_gather(permute_features(w_out), XZ + ("core",), axis=0, tiled=True)
    out_full = lax.dynamic_index_in_dim(
        out_rows.reshape(4, 2, HEAD_DIM, D), core, axis=1, keepdims=False
    ).reshape(HD, D)
    gate_full = gather_weight(part_gate)
    up_full = gather_weight(part_up)
    down_full = gather_weight(part_down)

    small = jnp.concatenate([ln1_gain, ln1_bias, ln2_gain, ln2_bias, qkv_bias])
    small = lax.all_gather(small, ROWS, axis=0, tiled=False)
    gain_one, bias_one, gain_two, bias_two = (
        permute_features(small[:, 16 * i : 16 * i + 16].reshape(D).astype(f32)) for i in range(4)
    )
    shift = small[:, 64:].reshape(3, 2, 4, HD)
    shift = lax.dynamic_index_in_dim(shift, core, axis=1, keepdims=False)
    shift = lax.dynamic_index_in_dim(shift, y, axis=1, keepdims=False).reshape(3 * HD).astype(f32)

    plan = jnp.concatenate([seq_lengths[0], slot_block[0]])
    plan = lax.all_gather(plan, "core", axis=0, tiled=False)
    blocks = plan[:, 2:].reshape(2, 2, 4)
    own_blocks = lax.dynamic_index_in_dim(blocks, zh, axis=1, keepdims=False)
    other_blocks = lax.dynamic_index_in_dim(blocks, 1 - zh, axis=1, keepdims=False)
    second, position, valid = jax.vmap(block_places)(
        plan[:, :2], jnp.concatenate([own_blocks, other_blocks], axis=1)
    )
    half = 4 * BLOCK
    q_second, q_position = second[:, :half], position[:, :half]
    allowed = (
        (q_second[:, :, None] == second[:, None, :])
        & (position[:, None, :] <= q_position[:, :, None])
        & valid[:, None, :]
    )
    cosine, sines = rotary_tables(q_position)
    own_valid = lax.dynamic_index_in_dim(
        lax.dynamic_index_in_dim(valid[:, :half].reshape(2, 4, BLOCK), core, 0, False), y, 0, False
    )

    hidden = permute_features(hidden_in[0]).astype(f32)
    grad_out = permute_features(cotangent[0]) * own_valid[:, None].astype(bf)
    grad_out_all = gather_tokens(grad_out)

    normed_one, inv_one = layer_norm(hidden)
    lowered_one = (normed_one * gain_one + bias_one).astype(bf)
    one_all = gather_tokens(lowered_one)
    joined = mm(one_all, qkv_full) + shift
    joined = joined.reshape(2, half, 3, 4, HEAD_DIM)
    queries = rotate(joined[:, :, 0], cosine, sines, 1.0).astype(bf)
    own_keys = rotate(joined[:, :, 1], cosine, sines, 1.0).astype(bf)
    own_values = joined[:, :, 2].astype(bf)
    swap = [(0, 1), (1, 0)]
    own_kv = jnp.stack([own_keys, own_values])
    other_kv = lax.ppermute(own_kv, "zh", swap)
    keys, values = jnp.concatenate([own_kv, other_kv], axis=2)

    raw = jnp.einsum("gthd,gshd->ghts", queries, keys, preferred_element_type=f32) * SCALE
    scores = jnp.where(allowed[:, None], raw, NEG)
    highest = jnp.max(scores, axis=-1, keepdims=True)
    log_total = highest + jnp.log(jnp.sum(jnp.exp(scores - highest), axis=-1, keepdims=True))
    probs = jnp.exp(scores - log_total)
    weights = probs.astype(bf)
    mixed = jnp.einsum("ghts,gshd->gthd", weights, values, preferred_element_type=f32)
    attended = mixed.reshape(2 * half, HD).astype(bf)

    middle = hidden + scatter_tokens(mm(attended, out_full).astype(bf)).astype(f32)
    normed_two, inv_two = layer_norm(middle)
    lowered_two = (normed_two * gain_two + bias_two).astype(bf)
    two_all = gather_tokens(lowered_two)
    gate = mm(two_all, gate_full)
    up_proj = mm(two_all, up_full)
    sig = jax.nn.sigmoid(gate)
    activated = gate * sig
    inner = (activated * up_proj).astype(bf)
    hidden_out = (middle + scatter_tokens(mm_nt(inner, down_full).astype(bf)).astype(f32)).astype(bf)

    inner_grad = mm(grad_out_all, down_full)
    gate_grad = (inner_grad * up_proj * sig * (1.0 + gate * (1.0 - sig))).astype(bf)
    up_grad = (inner_grad * activated).astype(bf)
    two_grad = scatter_tokens(
        (mm_nt(gate_grad, gate_full) + mm_nt(up_grad, up_full)).astype(bf)
    ).astype(f32)
    middle_grad = grad_out.astype(f32) + norm_back(two_grad, normed_two, inv_two, gain_two)
    branch_grad = middle_grad.astype(bf)
    branch_all = gather_tokens(branch_grad)
    attended_grad = mm_nt(branch_all, out_full).astype(bf)

    gate_sum = scatter_grad(mm_tn(two_all, gate_grad))
    up_sum = scatter_grad(mm_tn(two_all, up_grad))
    down_sum = scatter_grad(mm_tn(grad_out_all, inner))
    out_part = mm_tn(attended, branch_all).astype(bf).reshape(4, 1, HEAD_DIM, D)
    own_plane = (jnp.arange(2) == core)[None, :, None, None]
    out_part = jnp.where(own_plane, out_part, jnp.zeros((), bf)).reshape(4 * 2 * HEAD_DIM, D)
    out_sum = lax.psum_scatter(out_part, XZ + ("core",), scatter_dimension=0, tiled=True)

    grad_heads = attended_grad.reshape(2, half, 4, HEAD_DIM)
    prob_grad = jnp.einsum("gthd,gshd->ghts", grad_heads, values, preferred_element_type=f32)
    score_grad = (
        probs * (prob_grad - jnp.sum(probs * prob_grad, axis=-1, keepdims=True))
    ).astype(bf)
    query_grad = jnp.einsum("ghts,gshd->gthd", score_grad, keys, preferred_element_type=f32) * SCALE
    key_part = (
        jnp.einsum("ghts,gthd->gshd", score_grad, queries, preferred_element_type=f32) * SCALE
    )
    value_part = jnp.einsum("ghts,gthd->gshd", weights, grad_heads, preferred_element_type=f32)
    kv_part = jnp.stack([key_part, value_part])
    kv_back = lax.ppermute(kv_part[:, :, half:].astype(bf), "zh", swap).astype(f32)
    key_grad, value_grad = kv_part[:, :, :half] + kv_back
    joined_grad = jnp.stack(
        [
            rotate(query_grad, cosine, sines, -1.0),
            rotate(key_grad, cosine, sines, -1.0),
            value_grad,
        ],
        axis=2,
    ).astype(bf).reshape(2 * half, 3 * HD)
    qkv_sum = scatter_grad(mm_tn(one_all, joined_grad))
    one_grad = scatter_tokens(mm_nt(joined_grad, qkv_full).astype(bf)).astype(f32)
    input_grad = middle_grad + norm_back(one_grad, normed_one, inv_one, gain_one)

    shift_part = jnp.sum(joined_grad.astype(f32), axis=0).reshape(3, 1, 1, HD)
    mine = ((jnp.arange(2) == core)[:, None] & (jnp.arange(4) == y)[None, :])[None, :, :, None]
    shift_part = jnp.where(mine, shift_part, 0.0).reshape(3 * D)
    terms = jnp.stack(
        [
            jnp.sum(one_grad * normed_one, axis=0),
            jnp.sum(one_grad, axis=0),
            jnp.sum(two_grad * normed_two, axis=0),
            jnp.sum(two_grad, axis=0),
        ]
    )
    terms = restore_features(terms).reshape(4, 128, 16).transpose(1, 0, 2).reshape(128, 64)
    small_sum = lax.psum_scatter(
        jnp.concatenate([terms, shift_part.reshape(128, 48)], axis=1).reshape(-1),
        ROWS,
        scatter_dimension=0,
        tiled=True,
    )

    def whole(g):
        return g.transpose(1, 0, 2).reshape(16, FF).astype(f32)

    qkv_grad = (
        qkv_sum.reshape(4, 2, 16, 3, HD).transpose(2, 3, 1, 0, 4).reshape(16, 3 * D).astype(f32)
    )
    return (
        restore_features(hidden_out)[None],
        restore_features(input_grad)[None],
        small_sum[:16],
        small_sum[16:32],
        qkv_grad,
        small_sum[64:],
        restore_features(out_sum.astype(f32)),
        small_sum[32:48],
        small_sum[48:64],
        whole(gate_sum),
        whole(up_sum),
        whole(down_sum),
    )


def solution(mesh):
    inner = Mesh(mesh.devices.reshape(2, 4, 4, 2, 2), ROWS)
    rows = P(ROWS)
    tokens = P(GRP, SLOT, None)
    placed = (
        tokens,
        tokens,
        P(GRP, None),
        P(GRP, None),
        rows,
        rows,
        P(ROWS, None),
        rows,
        P(ROWS, None),
        rows,
        rows,
        P(ROWS, None),
        P(ROWS, None),
        P(ROWS, None),
    )
    return jax.shard_map(
        body,
        mesh=inner,
        in_specs=placed,
        out_specs=(
            tokens,
            tokens,
            rows,
            rows,
            P(ROWS, None),
            rows,
            P(ROWS, None),
            rows,
            rows,
            P(ROWS, None),
            P(ROWS, None),
            P(ROWS, None),
        ),
        check_vma=False,
    )
```

time: 3860 us -> 1200 us (0.31)
  waiting for transfers between devices: 3230 us -> 720 us
  matrix products: 251 us -> 128 us
  other arithmetic: 161 us -> 41.4 us
    reduce_scatter x2 -> x9, waiting for transfers between devices: 1980 us -> 473 us  [the longest x4 205 us: scatter_grad(): lax.psum_scatter(g.astype(jnp.bfloat16), XZ, scatter_dimension=0, tiled=T...]
    all_gather x7 -> x9, waiting for transfers between devices: 1110 us -> 214 us  [the longest x4 107 us: gather_weight(): return lax.all_gather(w, XZ, axis=0, tiled=True)]
    unnamed x13 -> x18, waiting for transfers between devices: 137 us -> 0.3 us
    concatenate x5 -> x2, other arithmetic: 134 us -> 1.48 us  [the longest x1 1.47 us: body(): keys, values = jnp.concatenate([own_kv, other_kv], axis=2)]
    dot_general x21, matrix products: 251 us -> 128 us  [the longest x5 37.7 us: mm(): return jnp.dot(a, b, preferred_element_type=jnp.float32)]
    all_to_all x0 -> x4, blocking collectives: none -> 41 us  [gather_weight(): w = lax.all_to_all(w, TPA, 0, 0, tiled=True).reshape(BLOCK, -1)]
    unnamed x2 -> x3, blocking collectives: 140 us -> 134 us
  transfers between devices with their start and end apart: 11 -> 24, of which waited for: 11 -> 18; matrix products, arithmetic and copies ran while one was open for 7% -> 16% of each run, Pallas kernels for 0% -> 0%
where the time goes in v1:
time: 1200 us; the launch traced here: 1190 us
  waiting for transfers between devices  720 us (60%)
  blocking collectives  175 us (15%)
  matrix products  128 us (11%)
  local copies, waits for them, and re-layouts  77 us (6%)
  other arithmetic  41.4 us (3%)
  starting transfers between devices  33.5 us (3%)
  between operations  16.3 us (1%)
    reduce_scatter x4, waiting for transfers between devices, scatter_grad(): lax.psum_scatter(g.astype(jnp.bfloat16), XZ, scatter_dimension=0, tiled=T...  205 us
    reduce_scatter x4, waiting for transfers between devices, scatter_tokens(): return lax.psum_scatter(v, TOK, scatter_dimension=0, tiled=True)  194 us
    unnamed x3, blocking collectives  134 us
    all_gather x4, waiting for transfers between devices, gather_weight(): return lax.all_gather(w, XZ, axis=0, tiled=True)  107 us
    all_gather x4, waiting for transfers between devices, gather_tokens(): return lax.all_gather(v, TOK, axis=0, tiled=True)  90.9 us
    reduce_scatter x1, waiting for transfers between devices, body(): lax.psum_scatter(out_part, XZ + ('core',), scatter_dimension=0, tiled=True)  74.8 us
    all_to_all x4, blocking collectives, gather_weight(): w = lax.all_to_all(w, TPA, 0, 0, tiled=True).reshape(BLOCK, -1)  41 us
    dot_general x5, matrix products, mm(): return jnp.dot(a, b, preferred_element_type=jnp.float32)  37.7 us
  transfers between devices with their start and end apart: 24, of which 18 were waited for; matrix products, arithmetic and copies ran while one was open for 16% of the time, Pallas kernels for 0%

profile of v1, /device:TPU:1, one launch (start us, length us, event | category | flops | bytes accessed | tf_op | source)
XLA Modules:
  0.0 1192.1 jit_solution(12408642629843224834)
XLA Ops:
  8.7 11.8 all_to_all.40
  24.2 67.0 %all-reduce = bf16[14336]{0:T(1024)(128)(2,1)S(1)} all-reduce(bf16[14336]{0:T(1024)(128)(2,1)S(1)} %dynamic-update-slice), channel_id=2, replica_groups=mesh['zh'=2,'y'=4,'x'=4,'zl'=2,'core'=2] {'zh','y','x','zl','core'}, use_global_device_ids=true, to_apply=%add | all-reduce | flops 14336 | bytes 57344
  103.3 23.1 %all-gather.12.cloned.1.call-done = bf16[1024,2048]{1,0:T(8,128)(2,1)} async-done(((bf16[128,2048]{1,0:T(8,128)(2,1)}), bf16[1024,2048]{1,0:T(8,128)(2,1)}) %all-gather.12.cloned.1.call-update) | async-done | bytes 4194320 | tf_op jit(solution)/shard_map/all_gather | solution.py:111
  126.4 8.2 convolution_add_fusion
  160.5 16.6 %all-gather.16.cloned.1.call-done = bf16[512,2048]{1,0:T(8,128)(2,1)} async-done(((bf16[16,2048]{1,0:T(8,128)(2,1)}), bf16[512,2048]{1,0:T(8,128)(2,1)}) %all-gather.16.cloned.1.call-update) | async-done | bytes 2097168 | tf_op jit(solution)/shard_map/all_gather | solution.py:145
  210.2 10.0 all_to_all.41
  220.7 45.6 %reduce-scatter.16.cloned.1.call-done = bf16[128,2048]{1,0:T(8,128)(2,1)} async-done(((bf16[1024,2048]{1,0:T(8,128)(2,1)}), bf16[128,2048]{1,0:T(8,128)(2,1)}) %reduce-scatter.16.cloned.1.call-update) | async-done | bytes 524304 | tf_op jit(solution)/shard_map/reduce_scatter | solution.py:115
  270.1 9.3 all_to_all.42
  279.8 9.9 all_to_all.43
  291.8 24.0 %all-gather.22.cloned.1.call-done = bf16[2048,704]{1,0:T(8,128)(2,1)} async-done(((bf16[128,704]{1,0:T(8,128)(2,1)}), bf16[2048,704]{1,0:T(8,128)(2,1)}) %all-gather.22.cloned.1.call-update) | async-done | bytes 2883600 | tf_op jit(solution)/shard_map/all_gather | solution.py:102
  315.8 33.8 %all-gather.18.cloned.1.call-done = bf16[1024,2048]{1,0:T(8,128)(2,1)} async-done(((bf16[128,2048]{1,0:T(8,128)(2,1)}), bf16[1024,2048]{1,0:T(8,128)(2,1)}) %all-gather.18.cloned.1.call-update) | async-done | bytes 4194320 | tf_op jit(solution)/shard_map/all_gather | solution.py:111
  349.7 7.9 fusion.44
  357.6 41.6 %all-gather.20.cloned.1.call-done = bf16[2048,704]{1,0:T(8,128)(2,1)} async-done(((bf16[128,704]{1,0:T(8,128)(2,1)}), bf16[2048,704]{1,0:T(8,128)(2,1)}) %all-gather.20.cloned.1.call-update) | async-done | bytes 2883600 | tf_op jit(solution)/shard_map/all_gather | solution.py:102
  399.2 7.9 fusion.43
  407.1 41.2 %all-gather.24.cloned.1.call-done = bf16[2048,704]{1,0:T(8,128)(2,1)} async-done(((bf16[128,704]{1,0:T(8,128)(2,1)}), bf16[2048,704]{1,0:T(8,128)(2,1)}) %all-gather.24.cloned.1.call-update) | async-done | bytes 2883600 | tf_op jit(solution)/shard_map/all_gather | solution.py:102
  448.3 34.0 %all-gather.26.cloned.1.call-done = bf16[1024,2048]{1,0:T(8,128)(2,1)} async-done(((bf16[128,2048]{1,0:T(8,128)(2,1)}), bf16[1024,2048]{1,0:T(8,128)(2,1)}) %all-gather.26.cloned.1.call-update) | async-done | bytes 4194320 | tf_op jit(solution)/shard_map/all_gather | solution.py:111
  482.3 10.5 multiply_convert_fusion.1
  501.8 7.8 convolution_convert_fusion
  509.7 43.9 %reduce-scatter.20.cloned.1.call-done = bf16[128,2048]{1,0:T(8,128)(2,1)} async-done(((bf16[1024,2048]{1,0:T(8,128)(2,1)}), bf16[128,2048]{1,0:T(8,128)(2,1)}) %reduce-scatter.20.cloned.1.call-update) | async-done | bytes 524304 | tf_op jit(solution)/shard_map/reduce_scatter | solution.py:115
  555.2 52.8 %reduce-scatter.18.cloned.1.call-done = bf16[128,2048]{1,0:T(8,128)(2,1)} async-done(((bf16[1024,2048]{1,0:T(8,128)(2,1)}), bf16[128,2048]{1,0:T(8,128)(2,1)}) %reduce-scatter.18.cloned.1.call-update) | async-done | bytes 524304 | tf_op jit(solution)/shard_map/reduce_scatter | solution.py:115
  611.2 7.4 convolution_convert_fusion.4
  656.2 13.1 %multiply_reduce_fusion = (f32[2,4,512]{2,1,0:T(4,128)S(1)}, f32[2,4,512,1024]{3,2,1,0:T(8,128)}) fusion(f32[2,4,512,1024]{3,2,1,0:T(8,128)} %copy-done, f32[2,4,512]{2,1,0:T(4,128)S(1)} %bitcast.216, pred[2,512,1024]{2,1,0:T(8,128)(4,1)S(1)} %and_and_fusion, bf16[2,512,4,64]{1,3,2,0:T(8,128)(2,1)} %copy.143, bf16[2,2,1024,4,64]{2,4,3,1,0:T(8,128)(2,1)S(1)} %copy-done.6), kind=kOutput, calls=%fused_computation.1 | convolution fusion | flops 557838336 | bytes 36208640 | tf_op jit(solution)/shard_map/gthd,gshd->ghts/dot_general | solution.py:239
  669.3 13.2 %multiply_convert_fusion = bf16[2,4,512,1024]{3,2,1,0:T(8,128)(2,1)S(1)} fusion(f32[2,4,512,1024]{3,2,1,0:T(8,128)} %get-tuple-element.104, f32[2,4,512,1024]{3,2,1,0:T(8,128)} %copy-done, f32[2,4,512]{2,1,0:T(4,128)S(1)} %get-tuple-element.103, f32[2,4,512]{2,1,0:T(4,128)S(1)} %bitcast.217, pred[2,512,1024]{2,1,0:T(8,128)(4,1)S(1)} %and_and_fusion), kind=kLoop, calls=%fused_computation | loop fusion | flops 25165824 | bytes 43024384 | tf_op jit(solution)/shard_map/convert_element_type | solution.py:242
  699.3 21.3 %collective-permute-done.1 = bf16[2,2,512,4,64]{2,4,3,1,0:T(8,128)(2,1)S(1)} collective-permute-done((bf16[2,2,512,4,64]{2,4,3,1,0:T(8,128)(2,1)S(1)}, bf16[2,2,512,4,64]{2,4,3,1,0:T(8,128)(2,1)S(1)}, u32[]{:S(2)}, u32[]{:S(2)}) %collective-permute-start.1) | collective-permute-done | bytes 1048608 | tf_op jit(solution)/shard_map/ppermute | solution.py:249
  735.0 7.0 convolution_convert_fusion.2
  747.8 71.6 %reduce-scatter.28.cloned.1.call-done = bf16[128,704]{1,0:T(8,128)(2,1)} async-done(((bf16[2048,704]{1,0:T(8,128)(2,1)}), bf16[128,704]{1,0:T(8,128)(2,1)}) %reduce-scatter.28.cloned.1.call-update) | async-done | bytes 180240 | tf_op jit(solution)/shard_map/reduce_scatter | solution.py:106
  827.2 70.5 %reduce-scatter.30.cloned.1.call-done = bf16[128,704]{1,0:T(8,128)(2,1)} async-done(((bf16[2048,704]{1,0:T(8,128)(2,1)}), bf16[128,704]{1,0:T(8,128)(2,1)}) %reduce-scatter.30.cloned.1.call-update) | async-done | bytes 180240 | tf_op jit(solution)/shard_map/reduce_scatter | solution.py:106
  897.7 6.8 all-to-all-start.6
  913.2 62.8 %reduce-scatter.24.cloned.1.call-done = bf16[128,768]{1,0:T(8,128)(2,1)} async-done(((bf16[2048,768]{1,0:T(8,128)(2,1)}), bf16[128,768]{1,0:T(8,128)(2,1)}) %reduce-scatter.24.cloned.1.call-update) | async-done | bytes 196624 | tf_op jit(solution)/shard_map/reduce_scatter | solution.py:106
  982.9 74.8 %reduce-scatter.26.cloned.1.call-done = bf16[16,2048]{1,0:T(8,128)(2,1)} async-done(((bf16[512,2048]{1,0:T(8,128)(2,1)}), bf16[16,2048]{1,0:T(8,128)(2,1)}) %reduce-scatter.26.cloned.1.call-update) | async-done | bytes 65552 | tf_op jit(solution)/shard_map/reduce_scatter | solution.py:236
  1061.9 51.2 %reduce-scatter.22.cloned.1.call-done = bf16[128,2048]{1,0:T(8,128)(2,1)} async-done(((bf16[1024,2048]{1,0:T(8,128)(2,1)}), bf16[128,2048]{1,0:T(8,128)(2,1)}) %reduce-scatter.22.cloned.1.call-update) | async-done | bytes 524304 | tf_op jit(solution)/shard_map/reduce_scatter | solution.py:115
  1115.4 65.2 %all-reduce.2 = f32[14336]{0:T(1024)S(1)} all-reduce(f32[14336]{0:T(1024)S(1)} %reshape.567), channel_id=8, replica_groups=mesh['zh'=2,'y'=4,'x'=4,'zl'=2,'core'=2] {'zh','y','x','zl','core'}, use_global_device_ids=true, to_apply=%region_20.21.clone | all-reduce | flops 14336 | bytes 114688
  (315 shorter events, 204.0 us)
Async XLA Ops:
  7.2 96.1 %all-gather.14.cloned.1.call-start = ((), (), s32[]{:S(2)}) async-start(), calls=%async_computation.18 | async-start | bytes 3342336 | tf_op jit(solution)/shard_map/all_gather | solution.py:102
  20.5 105.9 %all-gather.12.cloned.1.call-start = ((), (), s32[]{:S(2)}) async-start(), calls=%async_computation.17 | async-start | bytes 4718592 | tf_op jit(solution)/shard_map/all_gather | solution.py:111
  94.9 171.4 %copy-start.1 = (f32[128,2048]{1,0:T(8,128)}, f32[128,2048]{1,0:T(8,128)S(1)}, u32[]{:S(2)}) copy-start(f32[128,2048]{1,0:T(8,128)S(1)} %copy.131) | copy-start | bytes 3145732
  96.6 80.6 %all-gather.16.cloned.1.call-start = ((), (), s32[]{:S(2)}) async-start(), calls=%async_computation.19 | async-start | bytes 2162688 | tf_op jit(solution)/shard_map/all_gather | solution.py:145
  97.9 168.4 %reduce-scatter.16.cloned.1.call-start = ((), (), s32[]{:S(2)}) async-start(), calls=%async_computation.20 | async-start | bytes 4718592 | tf_op jit(solution)/shard_map/reduce_scatter | solution.py:115
  156.3 30.7 %collective-permute-start = (bf16[2,2,512,4,64]{2,4,3,1,0:T(8,128)(2,1)}, bf16[2,2,512,4,64]{2,4,3,1,0:T(8,128)(2,1)}, u32[]{:S(2)}, u32[]{:S(2)}) collective-permute-start(bf16[2,2,512,4,64]{2,4,3,1,0:T(8,128)(2,1)} %pad_maximum_fusion.2), channel_id=1, source_target_pairs={{0,64},{64,0},{1,65},{65,1},{2,66},{66,2},{3,67},{67,3},{4,68},{68... | collective-permute-start | bytes 3145736 | tf_op jit(solution)/shard_map/ppermute | solution.py:196
  160.5 508.8 %copy-start.3 = (pred[2,512,1024]{2,1,0:T(8,128)(4,1)}, pred[2,512,1024]{2,1,0:T(8,128)(4,1)S(1)}, u32[]{:S(2)}) copy-start(pred[2,512,1024]{2,1,0:T(8,128)(4,1)S(1)} %and_and_fusion) | copy-start | bytes 3145732
  209.1 106.7 %all-gather.22.cloned.1.call-start = ((), (), s32[]{:S(2)}) async-start(), calls=%async_computation.23 | async-start | bytes 3342336 | tf_op jit(solution)/shard_map/all_gather | solution.py:102
  220.3 129.4 %all-gather.18.cloned.1.call-start = ((), (), s32[]{:S(2)}) async-start(), calls=%async_computation.21 | async-start | bytes 4718592 | tf_op jit(solution)/shard_map/all_gather | solution.py:111
  268.9 130.3 %all-gather.20.cloned.1.call-start = ((), (), s32[]{:S(2)}) async-start(), calls=%async_computation.22 | async-start | bytes 3342336 | tf_op jit(solution)/shard_map/all_gather | solution.py:102
  279.5 168.8 %all-gather.24.cloned.1.call-start = ((), (), s32[]{:S(2)}) async-start(), calls=%async_computation.24 | async-start | bytes 3342336 | tf_op jit(solution)/shard_map/all_gather | solution.py:102
  289.7 192.6 %all-gather.26.cloned.1.call-start = ((), (), s32[]{:S(2)}) async-start(), calls=%async_computation.26 | async-start | bytes 4718592 | tf_op jit(solution)/shard_map/all_gather | solution.py:111
  291.3 262.3 %reduce-scatter.20.cloned.1.call-start = ((), (), s32[]{:S(2)}) async-start(), calls=%async_computation.27 | async-start | bytes 4718592 | tf_op jit(solution)/shard_map/reduce_scatter | solution.py:115
  501.7 106.2 %reduce-scatter.18.cloned.1.call-start = ((), (), s32[]{:S(2)}) async-start(), calls=%async_computation.25 | async-start | bytes 4718592 | tf_op jit(solution)/shard_map/reduce_scatter | solution.py:115
  509.6 137.1 %all-gather.28.cloned.1.call-start = ((), (), s32[]{:S(2)}) async-start(), calls=%async_computation.28 | async-start | bytes 4718592 | tf_op jit(solution)/shard_map/all_gather | solution.py:111
  611.1 131.0 %reduce-scatter.32.cloned.1.call-start = ((), (), s32[]{:S(2)}) async-start(), calls=%async_computation.34 | async-start | bytes 3342336 | tf_op jit(solution)/shard_map/reduce_scatter | solution.py:106
  623.4 196.0 %reduce-scatter.28.cloned.1.call-start = ((), (), s32[]{:S(2)}) async-start(), calls=%async_computation.32 | async-start | bytes 3342336 | tf_op jit(solution)/shard_map/reduce_scatter | solution.py:106
  634.8 262.9 %reduce-scatter.30.cloned.1.call-start = ((), (), s32[]{:S(2)}) async-start(), calls=%async_computation.33 | async-start | bytes 3342336 | tf_op jit(solution)/shard_map/reduce_scatter | solution.py:106
  646.4 329.6 %reduce-scatter.24.cloned.1.call-start = ((), (), s32[]{:S(2)}) async-start(), calls=%async_computation.30 | async-start | bytes 3342336 | tf_op jit(solution)/shard_map/reduce_scatter | solution.py:106
  693.4 27.2 %collective-permute-start.1 = (bf16[2,2,512,4,64]{2,4,3,1,0:T(8,128)(2,1)S(1)}, bf16[2,2,512,4,64]{2,4,3,1,0:T(8,128)(2,1)S(1)}, u32[]{:S(2)}, u32[]{:S(2)}) collective-permute-start(bf16[2,2,512,4,64]{2,4,3,1,0:T(8,128)(2,1)S(1)} %fusion.5), channel_id=1, source_target_pairs={{0,64},{64,0},{1,65},{65,1},{2,66},{66,2},{3,67},{67,3},{4,68},{68... | collective-permute-start | bytes 3145736 | tf_op jit(solution)/shard_map/ppermute | solution.py:249
  728.8 328.9 %reduce-scatter.26.cloned.1.call-start = ((), (), s32[]{:S(2)}) async-start(), calls=%async_computation.31 | async-start | bytes 2162688 | tf_op jit(solution)/shard_map/reduce_scatter | solution.py:236
  735.0 378.0 %reduce-scatter.22.cloned.1.call-start = ((), (), s32[]{:S(2)}) async-start(), calls=%async_computation.29 | async-start | bytes 4718592 | tf_op jit(solution)/shard_map/reduce_scatter | solution.py:115
  742.1 77.3 %all-to-all-start.7 = ((bf16[8,16,704]{2,1,0:T(8,128)(2,1)}), bf16[8,16,704]{2,1,0:T(8,128)(2,1)S(1)}, u32[]{:S(2)}, u32[]{:S(2)}) async-start(bf16[8,16,704]{2,1,0:T(8,128)(2,1)} %bitcast.213), calls=%async_computation.13 | async-start | bytes 393216 | tf_op jit(solution)/shard_map/all_to_all | solution.py:107
  819.4 78.3 %all-to-all-start.5 = ((bf16[8,16,704]{2,1,0:T(8,128)(2,1)}), bf16[8,16,704]{2,1,0:T(8,128)(2,1)S(1)}, u32[]{:S(2)}, u32[]{:S(2)}) async-start(bf16[8,16,704]{2,1,0:T(8,128)(2,1)} %bitcast.212), calls=%async_computation.11 | async-start | bytes 393216 | tf_op jit(solution)/shard_map/all_to_all | solution.py:107
  826.1 85.6 %copy-start.16 = (bf16[128,2048]{1,0:T(8,128)(2,1)S(1)}, bf16[128,2048]{1,0:T(8,128)(2,1)}, u32[]{:S(2)}) copy-start(bf16[128,2048]{1,0:T(8,128)(2,1)} %get-tuple-element.81) | copy-start | bytes 1572868
  897.7 12.7 %all-to-all-start.6 = ((bf16[8,16,704]{2,1,0:T(8,128)(2,1)}), bf16[8,16,704]{2,1,0:T(8,128)(2,1)S(1)}, u32[]{:S(2)}, u32[]{:S(2)}) async-start(bf16[8,16,704]{2,1,0:T(8,128)(2,1)} %bitcast.211), calls=%async_computation.12 | async-start | bytes 393216 | tf_op jit(solution)/shard_map/all_to_all | solution.py:107
  912.1 200.9 %copy-start.2 = (f32[128,2048]{1,0:T(8,128)S(1)}, f32[128,2048]{1,0:T(8,128)}, u32[]{:S(2)}) copy-start(f32[128,2048]{1,0:T(8,128)} %copy-done.1) | copy-start | bytes 3145732
  912.1 200.9 %copy-start.26 = (f32[2048]{0:T(1024)S(1)}, f32[2048]{0:T(1024)}, u32[]{:S(2)}) copy-start(f32[2048]{0:T(1024)} %copy-done.25) | copy-start | bytes 24580
  912.1 200.9 %copy-start.30 = (f32[128]{0:T(128)S(1)}, f32[128]{0:T(128)}, u32[]{:S(2)}) copy-start(f32[128]{0:T(128)} %copy-done.29) | copy-start | bytes 1540
  912.1 200.9 %copy-start.32 = (f32[128]{0:T(128)S(1)}, f32[128]{0:T(128)}, u32[]{:S(2)}) copy-start(f32[128]{0:T(128)} %copy-done.31) | copy-start | bytes 1540
  976.0 84.4 %all-to-all-start.4 = ((bf16[8,16,768]{2,1,0:T(8,128)(2,1)}), bf16[8,16,768]{2,1,0:T(8,128)(2,1)S(1)}, u32[]{:S(2)}, u32[]{:S(2)}) async-start(bf16[8,16,768]{2,1,0:T(8,128)(2,1)} %bitcast.214), calls=%async_computation.9 | async-start | bytes 393216 | tf_op jit(solution)/shard_map/all_to_all | solution.py:107
  1059.1 122.7 %copy-start.9 = (f32[128,2048]{1,0:T(8,128)S(1)}, f32[128,2048]{1,0:T(8,128)}, u32[]{:S(2)}) copy-start(f32[128,2048]{1,0:T(8,128)} %get-tuple-element.62) | copy-start | bytes 3145732
  (39 other events, 541.8 us)
Sparse Core Ops, SparseCore 0:
  20.6 48.8 all-gather.13
  96.7 29.6 all-gather.11
  129.2 47.8 all-gather.15
  209.2 57.0 reduce-scatter.15
  268.4 47.4 all-gather.21
  318.0 31.6 all-gather.17
  351.9 47.2 all-gather.19
  401.4 46.8 all-gather.23
  450.6 31.6 all-gather.25
  501.8 51.7 reduce-scatter.19
  556.0 51.8 reduce-scatter.17
  611.2 32.1 all-gather.27
  646.8 94.2 reduce-scatter.31
  744.3 75.0 reduce-scatter.27
  822.6 75.0 reduce-scatter.29
  900.9 75.0 reduce-scatter.23
  979.4 78.1 reduce-scatter.25
  1059.9 53.0 reduce-scatter.21

commit v2 on v1

v2 whole, which is shorter than its diff:
```python
import functools

import jax
import jax.numpy as jnp
from jax import lax
from jax.experimental import pallas as pl
from jax.experimental.pallas import tpu as pltpu
from jax.sharding import Mesh
from jax.sharding import PartitionSpec as P

D = 2048
HEADS = 32
HEAD_DIM = 64
ROT = 16
FF = 5632
BLOCK = 128
TP = 8
HD = D // TP
FC = FF // TP

EPS = 1e-05
NEG = -1e30
SCALE = HEAD_DIM ** (-0.5)
TPA = ("y", "core")
XZ = ("x", "zh", "zl")
ROWS = ("zh", "y", "x", "zl", "core")
GRP = ("x", "zl", "core")
SLOT = ("zh", "y")


def permute_features(v):
    lead = v.shape[:-1]
    n = len(lead)
    v = v.reshape(lead + (2, 4, 4, 2, 32))
    v = v.transpose(tuple(range(n)) + (n + 2, n, n + 3, n + 1, n + 4))
    return v.reshape(lead + (D,))


def restore_features(v):
    lead = v.shape[:-1]
    n = len(lead)
    v = v.reshape(lead + (4, 2, 2, 4, 32))
    v = v.transpose(tuple(range(n)) + (n + 1, n + 3, n, n + 2, n + 4))
    return v.reshape(lead + (D,))


def block_places(lengths, blocks):
    first_pad = (lengths[0] + BLOCK - 1) // BLOCK * BLOCK
    offsets = jnp.arange(BLOCK, dtype=jnp.int32)
    placed = (blocks[:, None] * BLOCK + offsets[None, :]).reshape(-1)
    second = (placed >= first_pad).astype(jnp.int32)
    position = placed - second * first_pad
    limit = jnp.where(second == 1, lengths[1], lengths[0])
    return second, position, position < limit


def rotary_tables(position):
    freq_steps = jnp.arange(ROT // 2, dtype=jnp.float32)
    inverse = 10000.0 ** (-2.0 * freq_steps / ROT)
    phases = position.astype(jnp.float32)[..., None] * inverse
    return jnp.cos(phases), jnp.sin(phases)


def rotate(shaped, cosine, sines, direction):
    half = ROT // 2
    front = shaped[..., :half]
    behind = shaped[..., half:ROT]
    c = cosine[:, :, None, :]
    s = sines[:, :, None, :] * direction
    return jnp.concatenate(
        [front * c - behind * s, behind * c + front * s, shaped[..., ROT:]], axis=-1
    )


def layer_norm(values):
    average = jnp.mean(values, axis=-1, keepdims=True)
    centred = values - average
    inv_scale = lax.rsqrt(jnp.mean(centred * centred, axis=-1, keepdims=True) + EPS)
    return centred * inv_scale, inv_scale


def norm_back(grad_in, normed, inv_scale, gain):
    scaled = grad_in * gain
    return inv_scale * (
        scaled
        - jnp.mean(scaled, axis=-1, keepdims=True)
        - normed * jnp.mean(scaled * normed, axis=-1, keepdims=True)
    )


def mm(a, b):
    return jnp.dot(a, b, preferred_element_type=jnp.float32)


def mm_nt(a, b):
    return lax.dot_general(a, b, (((1,), (1,)), ((), ())), preferred_element_type=jnp.float32)


def mm_tn(a, b):
    return lax.dot_general(a, b, (((0,), (0,)), ((), ())), preferred_element_type=jnp.float32)


FP = 768
HALF = BLOCK // 2
ANY = pl.BlockSpec(memory_space=pl.ANY)
VM = pl.BlockSpec(memory_space=pltpu.VMEM)
BF = jnp.bfloat16
F32 = jnp.float32


def params(cid):
    return pltpu.CompilerParams(
        collective_id=cid, has_side_effects=True, vmem_limit_bytes=56 * 1024 * 1024
    )


def meet(peers):
    barrier = pltpu.get_barrier_semaphore()
    for peer in peers:
        pl.semaphore_signal(
            barrier, inc=1, device_id=peer, device_id_type=pl.DeviceIdType.MESH
        )
    pl.semaphore_wait(barrier, len(peers))


def remote(sems, i, src, dst, peer):
    return pltpu.make_async_remote_copy(
        src_ref=src,
        dst_ref=dst,
        send_sem=sems[0].at[i],
        recv_sem=sems[1].at[i],
        device_id=peer,
        device_id_type=pl.DeviceIdType.MESH,
    )


def ring():
    y = lax.axis_index("y")
    c = lax.axis_index("core")
    up = lax.rem(y + 1, 4)
    opp = lax.rem(y + 2, 4)
    dn = lax.rem(y + 3, 4)
    return y, c, up, opp, dn


def ring_peers(up, dn, c):
    return {"y": up}, {"y": dn}, {"core": 1 - c}


N_AG = 11
N_RS = 10


def ring_gather(own, full, local_sem, sems):
    y, c, up, opp, dn = ring()
    to_up, to_dn, to_sib = ring_peers(up, dn, c)
    first, last = pl.ds(0, HALF), pl.ds(HALF, HALF)
    cp = functools.partial(remote, sems)
    up1 = cp(0, own.at[first], full.at[y, c, first], to_up)
    dn1 = cp(1, own.at[last], full.at[y, c, last], to_dn)
    up2 = cp(2, own.at[last], full.at[y, c, last], to_up)
    dn2 = cp(3, own.at[first], full.at[y, c, first], to_dn)
    sib0 = cp(4, own, full.at[y, c], to_sib)
    here = pltpu.make_async_copy(own, full.at[y, c], local_sem)
    for one in (up1, dn1, up2, dn2, sib0, here):
        one.start()
    up1.wait_recv()
    far1 = cp(5, full.at[dn, c, first], full.at[dn, c, first], to_up)
    far1.start()
    dn1.wait_recv()
    far2 = cp(6, full.at[up, c, last], full.at[up, c, last], to_dn)
    far2.start()
    up2.wait_recv()
    sib1 = cp(7, full.at[dn, c], full.at[dn, c], to_sib)
    sib1.start()
    dn2.wait_recv()
    sib2 = cp(8, full.at[up, c], full.at[up, c], to_sib)
    sib2.start()
    far1.wait_recv()
    sib3 = cp(9, full.at[opp, c, first], full.at[opp, c, first], to_sib)
    sib3.start()
    far2.wait_recv()
    sib4 = cp(10, full.at[opp, c, last], full.at[opp, c, last], to_sib)
    sib4.start()
    for one in (sib0, sib1, sib2, sib3, sib4):
        one.wait_recv()
    here.wait()
    for one in (up1, dn1, up2, dn2, sib0, far1, far2, sib1, sib2, sib3, sib4):
        one.wait_send()


def rows_loop(count, step, body):
    @pl.loop(0, count // step)
    def _(i):
        body(pl.ds(pl.multiple_of(i * step, step), step))


RS_SCRATCH = [
    pltpu.VMEM((4, 2, BLOCK, D), F32),
    pltpu.VMEM((4, BLOCK, D), BF),
    pltpu.VMEM((4, BLOCK, D), BF),
    pltpu.VMEM((2, HALF, D), BF),
    pltpu.VMEM((2, HALF, D), BF),
    pltpu.VMEM((2, BLOCK, D), BF),
    pltpu.VMEM((2, BLOCK, D), BF),
    pltpu.SemaphoreType.DMA((N_RS,)),
    pltpu.SemaphoreType.DMA((N_RS,)),
]


def ring_scatter(partial, scratch):
    part, sib_out, sib_in, far_out, far_in, near_out, near_in, *sems = scratch
    y, c, up, opp, dn = ring()
    to_up, to_dn, to_sib = ring_peers(up, dn, c)
    first, last = pl.ds(0, HALF), pl.ds(HALF, HALF)
    cp = functools.partial(remote, sems)
    order = (opp, up, dn, y)
    sib = [cp(j, sib_out.at[j], sib_in.at[j], to_sib) for j in range(4)]

    def produce(j):
        partial(order[j], part.at[j])

        def lower(r):
            sib_out[j, r, :] = part[j, 1 - c, r, :].astype(BF)

        rows_loop(BLOCK, 32, lower)
        sib[j].start()

    far = [
        cp(4, far_out.at[0], far_in.at[0], to_up),
        cp(5, far_out.at[1], far_in.at[1], to_dn),
    ]
    near_early = [
        cp(6, near_out.at[0, last], near_in.at[0, last], to_up),
        cp(7, near_out.at[1, first], near_in.at[1, first], to_dn),
    ]
    near_late = [
        cp(8, near_out.at[0, first], near_in.at[0, first], to_up),
        cp(9, near_out.at[1, last], near_in.at[1, last], to_dn),
    ]
    produce(0)
    produce(1)
    sib[0].wait_recv()
    for k in range(2):

        def add_far(r, k=k):
            q = pl.ds(k * HALF + r.start, r.size)
            far_out[k, r, :] = (part[0, c, q, :] + sib_in[0, q, :].astype(F32)).astype(BF)

        rows_loop(HALF, 32, add_far)
        far[k].start()
    produce(2)
    for k in range(2):
        sib[1 + k].wait_recv()

        def add_near(r, k=k):
            q = pl.ds((1 - k) * HALF + r.start, r.size)
            near_out[k, q, :] = (part[1 + k, c, q, :] + sib_in[1 + k, q, :].astype(F32)).astype(BF)

        rows_loop(HALF, 32, add_near)
        near_early[k].start()
    produce(3)
    for k in range(2):
        far[k].wait_recv()

        def add_late(r, k=k):
            q = pl.ds(k * HALF + r.start, r.size)
            near_out[k, q, :] = (
                part[1 + k, c, q, :] + sib_in[1 + k, q, :].astype(F32) + far_in[k, r, :].astype(F32)
            ).astype(BF)

        rows_loop(HALF, 32, add_late)
        near_late[k].start()
    sib[3].wait_recv()
    for one in near_early + near_late:
        one.wait_recv()

    def finish(r):
        part[3, c, r, :] = (
            part[3, c, r, :]
            + sib_in[3, r, :].astype(F32)
            + near_in[0, r, :].astype(F32)
            + near_in[1, r, :].astype(F32)
        )

    rows_loop(BLOCK, 32, finish)
    for one in sib + far + near_early + near_late:
        one.wait_send()
    return part.at[3, c]


AG_SCRATCH = [
    pltpu.VMEM((BLOCK, D), BF),
    pltpu.SemaphoreType.DMA,
    pltpu.SemaphoreType.DMA((N_AG,)),
    pltpu.SemaphoreType.DMA((N_AG,)),
]
FULL = jax.ShapeDtypeStruct((4, 2, BLOCK, D), BF)


def kernel_norm_gather(hidden, gains, full, own, local_sem, *sems):
    y, c, up, opp, dn = ring()
    meet(ring_peers(up, dn, c))

    def norm(r):
        normed, _ = layer_norm(hidden[r, :].astype(F32))
        own[r, :] = (normed * gains[0:1, :] + gains[1:2, :]).astype(BF)

    rows_loop(BLOCK, 16, norm)
    ring_gather(own, full, local_sem, sems)


def norm_gather(hidden, gains, cid):
    return pl.pallas_call(
        kernel_norm_gather,
        out_shape=FULL,
        in_specs=[VM, VM],
        out_specs=ANY,
        scratch_shapes=AG_SCRATCH,
        compiler_params=params(cid),
        name="norm_gather",
    )(hidden, gains)


NT = (((1,), (1,)), ((), ()))


def kernel_out_proj(attended, weight, hidden, gains, middle, full, *scratch):
    own, local_sem, *sems = scratch[:4]
    y, c, up, opp, dn = ring()
    meet(ring_peers(up, dn, c))

    def partial(block, out):
        a = attended[block].reshape(2 * BLOCK, HD)

        @pl.loop(0, 4)
        def _(i):
            q = pl.ds(pl.multiple_of(i * 512, 512), 512)
            out[:, :, q] = jnp.dot(a, weight[:, q], preferred_element_type=F32).reshape(
                2, BLOCK, 512
            )

    total = ring_scatter(partial, scratch[4:])

    def norm(r):
        row = hidden[r, :].astype(F32) + total[r, :]
        middle[r, :] = row
        normed, _ = layer_norm(row)
        own[r, :] = (normed * gains[2:3, :] + gains[3:4, :]).astype(BF)

    rows_loop(BLOCK, 16, norm)
    ring_gather(own, full, local_sem, sems)


def out_proj(attended, weight, hidden, gains, cid):
    return pl.pallas_call(
        kernel_out_proj,
        out_shape=(jax.ShapeDtypeStruct((BLOCK, D), F32), FULL),
        in_specs=[VM] * 4,
        out_specs=(VM, ANY),
        scratch_shapes=AG_SCRATCH + RS_SCRATCH,
        compiler_params=params(cid),
        name="out_proj",
    )(attended, weight, hidden, gains)


def kernel_mlp_back(
    gate_grad, up_grad, w_gate, w_up, middle, grad_out, gains, middle_grad, sums, full, *scratch
):
    own, local_sem, *sems = scratch[:4]
    y, c, up, opp, dn = ring()
    meet(ring_peers(up, dn, c))

    def partial(block, out):
        a = gate_grad[block].reshape(2 * BLOCK, FP)
        b = up_grad[block].reshape(2 * BLOCK, FP)

        @pl.loop(0, 4)
        def _(i):
            q = pl.ds(pl.multiple_of(i * 512, 512), 512)
            out[:, :, q] = (
                lax.dot_general(a, w_gate[q, :], NT, preferred_element_type=F32)
                + lax.dot_general(b, w_up[q, :], NT, preferred_element_type=F32)
            ).reshape(2, BLOCK, 512)

    total = ring_scatter(partial, scratch[4:])
    sums[...] = jnp.zeros_like(sums)

    def back(r):
        row = total[r, :]
        normed, inv = layer_norm(middle[r, :])
        grad = grad_out[r, :].astype(F32) + norm_back(row, normed, inv, gains[2:3, :])
        middle_grad[r, :] = grad
        own[r, :] = grad.astype(BF)
        sums[0:1, :] += jnp.sum(row * normed, axis=0, keepdims=True)
        sums[1:2, :] += jnp.sum(row, axis=0, keepdims=True)

    rows_loop(BLOCK, 16, back)
    ring_gather(own, full, local_sem, sems)


def mlp_back(gate_grad, up_grad, w_gate, w_up, middle, grad_out, gains, cid):
    return pl.pallas_call(
        kernel_mlp_back,
        out_shape=(
            jax.ShapeDtypeStruct((BLOCK, D), F32),
            jax.ShapeDtypeStruct((8, D), F32),
            FULL,
        ),
        in_specs=[VM] * 7,
        out_specs=(VM, VM, ANY),
        scratch_shapes=AG_SCRATCH + RS_SCRATCH,
        compiler_params=params(cid),
        name="mlp_back",
    )(gate_grad, up_grad, w_gate, w_up, middle, grad_out, gains)


def kernel_qkv_back(joined_grad, weight, hidden, middle_grad, gains, input_grad, sums, *scratch):
    y, c, up, opp, dn = ring()
    meet(ring_peers(up, dn, c))

    def partial(block, out):
        a = joined_grad[block].reshape(2 * BLOCK, 3 * HD)

        @pl.loop(0, 4)
        def _(i):
            q = pl.ds(pl.multiple_of(i * 512, 512), 512)
            out[:, :, q] = lax.dot_general(
                a, weight[q, :], NT, preferred_element_type=F32
            ).reshape(2, BLOCK, 512)

    total = ring_scatter(partial, scratch)
    sums[...] = jnp.zeros_like(sums)

    def back(r):
        row = total[r, :]
        normed, inv = layer_norm(hidden[r, :].astype(F32))
        input_grad[r, :] = middle_grad[r, :] + norm_back(row, normed, inv, gains[0:1, :])
        sums[0:1, :] += jnp.sum(row * normed, axis=0, keepdims=True)
        sums[1:2, :] += jnp.sum(row, axis=0, keepdims=True)

    rows_loop(BLOCK, 16, back)


def qkv_back(joined_grad, weight, hidden, middle_grad, gains, cid):
    return pl.pallas_call(
        kernel_qkv_back,
        out_shape=(jax.ShapeDtypeStruct((BLOCK, D), F32), jax.ShapeDtypeStruct((8, D), F32)),
        in_specs=[VM] * 5,
        out_specs=(VM, VM),
        scratch_shapes=RS_SCRATCH,
        compiler_params=params(cid),
        name="qkv_back",
    )(joined_grad, weight, hidden, middle_grad, gains)


TP_STEPS = [(dy, dc) for dy in range(4) for dc in range(2) if (dy, dc) != (0, 0)]
XZ_STEPS = [(dx, dz) for dx in range(4) for dz in range(4) if (dx, dz) != (0, 0)]


def tp_peer(step):
    y = lax.rem(lax.axis_index("y") + step[0], 4)
    c = lax.rem(lax.axis_index("core") + step[1], 2)
    return {"y": y, "core": c}, y * 2 + c


def xz_peer(step):
    x = lax.rem(lax.axis_index("x") + step[0], 4)
    z = lax.rem(lax.axis_index("zh") * 2 + lax.axis_index("zl") + step[1], 4)
    return {"x": x, "zh": z // 2, "zl": lax.rem(z, 2)}, x * 4 + z


def meet_all(split):
    peers = [tp_peer(s)[0] for s in TP_STEPS] + [xz_peer(s)[0] for s in XZ_STEPS]
    barrier = pltpu.get_barrier_semaphore()
    for peer in peers:
        pl.semaphore_signal(
            barrier, inc=1, device_id=peer, device_id_type=pl.DeviceIdType.MESH
        )

    @pl.when(split)
    def _():
        pl.semaphore_signal(
            barrier, inc=1, device_id=swap_peer(), device_id_type=pl.DeviceIdType.MESH
        )

    pl.semaphore_wait(barrier, len(peers) + split.astype(jnp.int32))


def swap_peer():
    return {"zh": lax.axis_index("core"), "core": lax.axis_index("zh")}


def swap_start(split, src, dst, local_sem, sems, i):
    @pl.when(split)
    def _():
        remote(sems, i, src, dst, swap_peer()).start()

    @pl.when(jnp.logical_not(split))
    def _():
        pltpu.make_async_copy(src, dst, local_sem).start()


def swap_wait(split, src, dst, local_sem, sems, i):
    @pl.when(split)
    def _():
        remote(sems, i, src, dst, swap_peer()).wait()

    @pl.when(jnp.logical_not(split))
    def _():
        pltpu.make_async_copy(src, dst, local_sem).wait()


N_TP = len(TP_STEPS)
N_XZ = len(XZ_STEPS)


def kernel_spread(small, qkv, mlp, out, small_all, qkv_all, mlp_all, out_all, local, *sems):
    me = lax.axis_index("y") * 2 + lax.axis_index("core")
    xz = lax.axis_index("x") * 4 + lax.axis_index("zh") * 2 + lax.axis_index("zl")
    split = lax.axis_index("zh") != lax.axis_index("core")
    meet_all(split)
    cp = functools.partial(remote, sems)
    tiny, big = [], []
    for k, step in enumerate(TP_STEPS):
        peer, there = tp_peer(step)
        tiny.append(cp(k, small, small_all.at[xz, me], peer))
        big.append(cp(N_TP + k, qkv.at[there], qkv_all.at[me], peer))
        big.append(cp(2 * N_TP + k, mlp.at[there], mlp_all.at[:, me], peer))
    keep = [
        pltpu.make_async_copy(small, small_all.at[xz, me], local.at[0]),
        pltpu.make_async_copy(qkv.at[me], qkv_all.at[me], local.at[1]),
        pltpu.make_async_copy(mlp.at[me], mlp_all.at[:, me], local.at[2]),
    ]
    for one in tiny + keep:
        one.start()
    for one in big:
        one.start()
    swap_start(split, out, out_all, local.at[3], sems, 3 * N_TP + N_XZ)
    for one in tiny:
        one.wait()
    keep[0].wait()
    wide = []
    for k, step in enumerate(XZ_STEPS):
        peer, _ = xz_peer(step)
        wide.append(cp(3 * N_TP + k, small_all.at[xz], small_all.at[xz], peer))
    for one in wide:
        one.start()
    for one in wide + big + keep[1:]:
        one.wait()
    swap_wait(split, out, out_all, local.at[3], sems, 3 * N_TP + N_XZ)


def spread(small, qkv, mlp, out, cid):
    n = 3 * N_TP + N_XZ + 1
    return pl.pallas_call(
        kernel_spread,
        out_shape=(
            jax.ShapeDtypeStruct((16, TP, 1, 128), F32),
            jax.ShapeDtypeStruct((TP, 16, FP), BF),
            jax.ShapeDtypeStruct((3, TP, 16, FP), BF),
            jax.ShapeDtypeStruct((16, D), BF),
        ),
        in_specs=[ANY] * 4,
        out_specs=(ANY,) * 4,
        scratch_shapes=[
            pltpu.SemaphoreType.DMA((4,)),
            pltpu.SemaphoreType.DMA((n,)),
            pltpu.SemaphoreType.DMA((n,)),
        ],
        compiler_params=params(cid),
        name="spread",
    )(small, qkv, mlp, out)


def kernel_collect(
    terms, shift, qkv, mlp, out, small_all, qkv_all, mlp_all, out_all, terms_in, shift_in, own, local, *sems
):
    me = lax.axis_index("y") * 2 + lax.axis_index("core")
    xz = lax.axis_index("x") * 4 + lax.axis_index("zh") * 2 + lax.axis_index("zl")
    split = lax.axis_index("zh") != lax.axis_index("core")
    meet_all(split)
    cp = functools.partial(remote, sems)
    wide, big = [], []
    for k, step in enumerate(XZ_STEPS):
        peer, there = xz_peer(step)
        wide.append(cp(k, terms.at[there], terms_in.at[xz], peer))
        wide.append(cp(N_XZ + k, shift, shift_in.at[xz], peer))
    for k, step in enumerate(TP_STEPS):
        peer, there = tp_peer(step)
        big.append(cp(2 * N_XZ + k, qkv.at[there], qkv_all.at[me], peer))
        big.append(cp(2 * N_XZ + N_TP + k, mlp.at[:, there], mlp_all.at[me], peer))
    keep = [
        pltpu.make_async_copy(terms.at[xz], terms_in.at[xz], local.at[0]),
        pltpu.make_async_copy(shift, shift_in.at[xz], local.at[1]),
        pltpu.make_async_copy(qkv.at[me], qkv_all.at[me], local.at[2]),
        pltpu.make_async_copy(mlp.at[:, me], mlp_all.at[me], local.at[3]),
    ]
    for one in wide + keep:
        one.start()
    for one in big:
        one.start()
    last = 2 * N_XZ + 3 * N_TP
    swap_start(split, out, out_all, local.at[4], sems, last)
    for one in wide + keep[:2]:
        one.wait()
    own[0:8, :] = jnp.sum(terms_in[...], axis=0)
    own[8:16, :] = jnp.sum(shift_in[...], axis=0)
    tiny = []
    for k, step in enumerate(TP_STEPS):
        peer, _ = tp_peer(step)
        tiny.append(cp(2 * N_XZ + 2 * N_TP + k, own, small_all.at[me], peer))
    tiny.append(pltpu.make_async_copy(own, small_all.at[me], local.at[0]))
    for one in tiny:
        one.start()
    for one in tiny + big + keep[2:]:
        one.wait()
    swap_wait(split, out, out_all, local.at[4], sems, last)


def collect(terms, shift, qkv, mlp, out, cid):
    n = 2 * N_XZ + 3 * N_TP + 1
    return pl.pallas_call(
        kernel_collect,
        out_shape=(
            jax.ShapeDtypeStruct((TP, 16, 128), F32),
            jax.ShapeDtypeStruct((TP, 16, FP), BF),
            jax.ShapeDtypeStruct((TP, 3, 16, FP), BF),
            jax.ShapeDtypeStruct((16, D), BF),
        ),
        in_specs=[ANY] * 5,
        out_specs=(ANY,) * 4,
        scratch_shapes=[
            pltpu.VMEM((16, 8, 128), F32),
            pltpu.VMEM((16, 8, 128), F32),
            pltpu.VMEM((16, 128), F32),
            pltpu.SemaphoreType.DMA((5,)),
            pltpu.SemaphoreType.DMA((n,)),
            pltpu.SemaphoreType.DMA((n,)),
        ],
        compiler_params=params(cid),
        name="collect",
    )(terms, shift, qkv, mlp, out)


def body(
    hidden_in,
    cotangent,
    seq_lengths,
    slot_block,
    ln1_gain,
    ln1_bias,
    w_qkv,
    qkv_bias,
    w_out,
    ln2_gain,
    ln2_bias,
    w_gate,
    w_up,
    w_down,
):
    bf, f32 = BF, F32
    zh = lax.axis_index("zh")
    y = lax.axis_index("y")
    core = lax.axis_index("core")
    xz = lax.axis_index("x") * 4 + zh * 2 + lax.axis_index("zl")

    def by_part(w):
        w = w.reshape(-1, 3, 2, 4, 4, 2, 2, 16)
        w = jnp.concatenate([w[:, :2], w[:, 2:].swapaxes(5, 6)], axis=1)
        return w.transpose(3, 2, 0, 1, 4, 5, 6, 7).reshape(TP, -1, 3 * HD)

    part_qkv = by_part(w_qkv)
    part_mlp = jnp.stack(
        [
            jnp.pad(w.reshape(16, TP, FC).transpose(1, 0, 2), ((0, 0), (0, 0), (0, FP - FC)))
            for w in (w_gate, w_up, w_down)
        ],
        axis=1,
    )
    lengths = seq_lengths[0]
    small = jnp.concatenate(
        [
            ln1_gain.astype(f32),
            ln1_bias.astype(f32),
            ln2_gain.astype(f32),
            ln2_bias.astype(f32),
            qkv_bias.astype(f32),
            lengths.astype(f32),
            slot_block[0].astype(f32),
            jnp.zeros(6, f32),
        ]
    ).reshape(1, 128)
    small_all, qkv_rows, mlp_rows, out_rows = spread(
        small, part_qkv, part_mlp, permute_features(w_out), 0
    )
    out_rows = out_rows.reshape(16, 8, HD).swapaxes(0, 1).reshape(BLOCK, HD)
    attn_full = lax.all_gather(
        jnp.concatenate([qkv_rows.reshape(BLOCK, FP), out_rows], axis=1), XZ, axis=0, tiled=True
    )
    mlp_full = lax.all_gather(mlp_rows.reshape(3, BLOCK, FP), XZ, axis=0, tiled=False)
    qkv_full = attn_full[:, :FP]
    out_full = (
        attn_full[:, FP:].reshape(16, 8, 16, HD).transpose(0, 2, 1, 3).reshape(HD, D)
    )
    gate_full, up_full, down_full = (mlp_full[:, i].reshape(D, FP) for i in range(3))

    small_all = small_all.reshape(BLOCK, 128)
    gains = (
        jnp.concatenate([small_all[:, 16 * i : 16 * i + 16].reshape(1, D) for i in range(4)])
    )
    gains = jnp.pad(gains, ((0, 4), (0, 0)))
    natural = small_all[:, 64:112].reshape(4, 2, 2, 4, 2, 48).transpose(1, 3, 0, 2, 4, 5)
    shift = by_part(natural.reshape(1, 3 * D))
    shift = lax.dynamic_index_in_dim(shift, y * 2 + core, 0, False)

    plan = lax.dynamic_slice_in_dim(small_all, xz * TP + y * 2, 2, 0)[:, 112:122].astype(jnp.int32)
    blocks = plan[:, 2:].reshape(2, 2, 4)
    own_blocks = lax.dynamic_index_in_dim(blocks, zh, axis=1, keepdims=False)
    other_blocks = lax.dynamic_index_in_dim(blocks, 1 - zh, axis=1, keepdims=False)
    second, position, valid = jax.vmap(block_places)(
        plan[:, :2], jnp.concatenate([own_blocks, other_blocks], axis=1)
    )
    half = 4 * BLOCK
    q_second, q_position = second[:, :half], position[:, :half]
    allowed = (
        (q_second[:, :, None] == second[:, None, :])
        & (position[:, None, :] <= q_position[:, :, None])
        & valid[:, None, :]
    )
    cosine, sines = rotary_tables(q_position)
    place = (zh * 4 + y) * BLOCK
    _, _, slot_valid = block_places(lengths, slot_block[0])
    own_valid = lax.dynamic_slice_in_dim(slot_valid, place, BLOCK, 0)

    def by_group(v):
        return v.reshape(4, 2, BLOCK, -1).swapaxes(0, 1).reshape(2, half, -1)

    def by_token(v):
        return v.reshape(2, 4, BLOCK, -1).swapaxes(0, 1)

    hidden = permute_features(hidden_in[0])
    grad_out = permute_features(cotangent[0]) * own_valid[:, None].astype(bf)
    grad_out_all = lax.all_gather(grad_out, TPA, axis=0, tiled=True)

    one_all = norm_gather(hidden, gains, 1).reshape(TP * BLOCK, D)
    joined = by_group(mm(one_all, qkv_full) + shift).reshape(2, half, 3, 4, HEAD_DIM)
    queries = rotate(joined[:, :, 0], cosine, sines, 1.0).astype(bf)
    own_keys = rotate(joined[:, :, 1], cosine, sines, 1.0).astype(bf)
    own_values = joined[:, :, 2].astype(bf)
    swap = [(0, 1), (1, 0)]
    own_kv = jnp.stack([own_keys, own_values])
    other_kv = lax.ppermute(own_kv, "zh", swap)
    keys, values = jnp.concatenate([own_kv, other_kv], axis=2)

    raw = jnp.einsum("gthd,gshd->ghts", queries, keys, preferred_element_type=f32) * SCALE
    scores = jnp.where(allowed[:, None], raw, NEG)
    highest = jnp.max(scores, axis=-1, keepdims=True)
    log_total = highest + jnp.log(jnp.sum(jnp.exp(scores - highest), axis=-1, keepdims=True))
    probs = jnp.exp(scores - log_total)
    weights = probs.astype(bf)
    mixed = jnp.einsum("ghts,gshd->gthd", weights, values, preferred_element_type=f32)
    attended = by_token(mixed.reshape(2, half, HD).astype(bf))

    middle, two_all = out_proj(attended, out_full, hidden, gains, 2)
    two_all = two_all.reshape(TP * BLOCK, D)
    gate = mm(two_all, gate_full)
    up_proj = mm(two_all, up_full)
    sig = jax.nn.sigmoid(gate)
    activated = gate * sig
    inner = (activated * up_proj).astype(bf)
    hidden_out = lax.psum_scatter(
        mm_nt(inner, down_full).astype(bf), TPA, scatter_dimension=0, tiled=True
    )
    hidden_out = (middle + hidden_out.astype(f32)).astype(bf)

    inner_grad = mm(grad_out_all, down_full)
    gate_grad = (inner_grad * up_proj * sig * (1.0 + gate * (1.0 - sig))).astype(bf)
    up_grad = (inner_grad * activated).astype(bf)
    middle_grad, two_sums, branch_all = mlp_back(
        gate_grad.reshape(4, 2, BLOCK, FP),
        up_grad.reshape(4, 2, BLOCK, FP),
        gate_full,
        up_full,
        middle,
        grad_out,
        gains,
        3,
    )
    branch_all = branch_all.reshape(TP * BLOCK, D)
    attended_grad = mm_nt(branch_all, out_full).astype(bf)

    mlp_part = jnp.stack(
        [mm_tn(two_all, gate_grad), mm_tn(two_all, up_grad), mm_tn(grad_out_all, inner)], axis=0
    ).astype(bf)
    mlp_part = mlp_part.reshape(3, 16, BLOCK, FP).swapaxes(0, 1).reshape(-1, FP)
    mlp_sum = lax.psum_scatter(mlp_part, XZ, scatter_dimension=0, tiled=True)
    out_part = mm_tn(attended.reshape(TP * BLOCK, HD), branch_all).astype(bf)
    out_sum = lax.psum_scatter(out_part, XZ, scatter_dimension=0, tiled=True)

    grad_heads = by_group(attended_grad).reshape(2, half, 4, HEAD_DIM)
    prob_grad = jnp.einsum("gthd,gshd->ghts", grad_heads, values, preferred_element_type=f32)
    score_grad = (
        probs * (prob_grad - jnp.sum(probs * prob_grad, axis=-1, keepdims=True))
    ).astype(bf)
    query_grad = jnp.einsum("ghts,gshd->gthd", score_grad, keys, preferred_element_type=f32) * SCALE
    key_part = (
        jnp.einsum("ghts,gthd->gshd", score_grad, queries, preferred_element_type=f32) * SCALE
    )
    value_part = jnp.einsum("ghts,gthd->gshd", weights, grad_heads, preferred_element_type=f32)
    kv_part = jnp.stack([key_part, value_part])
    kv_back = lax.ppermute(kv_part[:, :, half:].astype(bf), "zh", swap).astype(f32)
    key_grad, value_grad = kv_part[:, :, :half] + kv_back
    joined_grad = jnp.stack(
        [
            rotate(query_grad, cosine, sines, -1.0),
            rotate(key_grad, cosine, sines, -1.0),
            value_grad,
        ],
        axis=2,
    ).astype(bf)
    joined_grad = by_token(joined_grad.reshape(2, half, 3 * HD))
    flat_grad = joined_grad.reshape(TP * BLOCK, 3 * HD)
    qkv_sum = lax.psum_scatter(
        mm_tn(one_all, flat_grad).astype(bf), XZ, scatter_dimension=0, tiled=True
    )
    input_grad, one_sums = qkv_back(joined_grad, qkv_full, hidden, middle_grad, gains, 4)

    terms = jnp.concatenate([one_sums[:2], two_sums[:2]]).reshape(4, 16, 128).swapaxes(0, 1)
    terms = jnp.pad(terms, ((0, 0), (0, 4), (0, 0)))
    shift_part = jnp.sum(flat_grad.astype(f32), axis=0).reshape(6, 128)
    shift_part = jnp.pad(shift_part, ((0, 2), (0, 0)))
    small_sum, qkv_all, mlp_all, out_all = collect(
        terms, shift_part, qkv_sum.reshape(TP, 16, FP), mlp_sum.reshape(3, TP, 16, FP), out_sum, 5
    )

    def restore_parts(g):
        g = g.reshape(4, 2, -1, 3, 4, 2, 2, 16).transpose(2, 3, 1, 0, 4, 5, 6, 7)
        g = jnp.concatenate([g[:, :2], g[:, 2:].swapaxes(5, 6)], axis=1)
        return g.reshape(-1, 3 * D)

    vectors = jnp.sum(small_sum[:, :4], axis=0)
    vectors = lax.dynamic_slice_in_dim(vectors, (y * 2 + core) * 16, 16, 1)
    shift_grad = restore_parts(small_sum[:, 8:14].reshape(TP, 1, FP)).reshape(128, 48)
    row = (zh * 4 + y) * 16 + lax.axis_index("x") * 4 + lax.axis_index("zl") * 2 + core
    shift_grad = lax.dynamic_index_in_dim(shift_grad, row, 0, False)

    def whole(i):
        return mlp_all[:, i, :, :FC].swapaxes(0, 1).reshape(16, FF).astype(f32)

    return (
        restore_features(hidden_out)[None],
        restore_features(input_grad)[None],
        vectors[0],
        vectors[1],
        restore_parts(qkv_all.astype(f32)),
        shift_grad,
        restore_features(out_all.astype(f32)),
        vectors[2],
        vectors[3],
        whole(0),
        whole(1),
        whole(2),
    )


def solution(mesh):
    inner = Mesh(mesh.devices.reshape(2, 4, 4, 2, 2), ROWS)
    rows = P(ROWS)
    tokens = P(GRP, SLOT, None)
    placed = (
        tokens,
        tokens,
        P(GRP, None),
        P(GRP, None),
        rows,
        rows,
        P(ROWS, None),
        rows,
        P(ROWS, None),
        rows,
        rows,
        P(ROWS, None),
        P(ROWS, None),
        P(ROWS, None),
    )
    return jax.shard_map(
        body,
        mesh=inner,
        in_specs=placed,
        out_specs=(
            tokens,
            tokens,
            rows,
            rows,
            P(ROWS, None),
            rows,
            P(ROWS, None),
            rows,
            rows,
            P(ROWS, None),
            P(ROWS, None),
            P(ROWS, None),
        ),
        check_vma=False,
    )
```

time: 1200 us -> 686 us (0.57)
  waiting for transfers between devices: 720 us -> 182 us
  Pallas kernels: 0 us -> 216 us
  blocking collectives: 175 us -> 0 us
  local copies, waits for them, and re-layouts: 77 us -> 110 us
  starting transfers between devices: 33.5 us -> 4.47 us
  matrix products: 128 us -> 99.3 us
    reduce_scatter x9 -> x4, waiting for transfers between devices: 473 us -> 122 us  [the longest x1 91.4 us: body(): mlp_sum = lax.psum_scatter(mlp_part, XZ, scatter_dimension=0, tiled=True)]
    pallas_call x0 -> x6, Pallas kernels: none -> 216 us  [the longest x1 64.7 us: mlp_back(): pl.pallas_call(kernel_mlp_back, out_shape=(jax.ShapeDtypeStruct((BLOCK, D...]
    all_gather x9 -> x3, waiting for transfers between devices: 214 us -> 12.2 us  [the longest x1 12.2 us: body(): lax.all_gather(jnp.concatenate([qkv_rows.reshape(BLOCK, FP), out_rows], a...]
    unnamed x3 -> x0, blocking collectives: 134 us -> none
    all_to_all x4 -> x0, blocking collectives: 41 us -> none  [gather_weight(): w = lax.all_to_all(w, TPA, 0, 0, tiled=True).reshape(BLOCK, -1)]
    all_to_all x4 -> x0, starting transfers between devices: 25.8 us -> none  [scatter_grad(): return lax.all_to_all(g.reshape(TP, 16, -1), TPA, 0, 0, tiled=True)]
    ppermute x1, waiting for transfers between devices: 6.35 us -> 26.2 us  [body(): other_kv = lax.ppermute(own_kv, 'zh', swap)]
    dot_general x5 -> x2, matrix products: 28 us -> 9.36 us  [mm_nt(): lax.dot_general(a, b, (((1,), (1,)), ((), ())), preferred_element_type=jn...]
  transfers between devices with their start and end apart: 24 -> 9, of which waited for: 18 -> 5; matrix products, arithmetic and copies ran while one was open for 16% -> 27% of each run, Pallas kernels for 0% -> 26%
where the time goes in v2:
time: 686 us; the launch traced here: 678 us
  Pallas kernels  216 us (31%)
  waiting for transfers between devices  182 us (27%)
  local copies, waits for them, and re-layouts  110 us (16%)
  matrix products  99.3 us (14%)
  other arithmetic  49.3 us (7%)
  between operations  16.2 us (2%)
    reduce_scatter x1, waiting for transfers between devices, body(): mlp_sum = lax.psum_scatter(mlp_part, XZ, scatter_dimension=0, tiled=True)  91.4 us
    pallas_call x1, Pallas kernels, mlp_back(): pl.pallas_call(kernel_mlp_back, out_shape=(jax.ShapeDtypeStruct((BLOCK, D...  64.7 us
    pallas_call x1, Pallas kernels, out_proj(): pl.pallas_call(kernel_out_proj, out_shape=(jax.ShapeDtypeStruct((BLOCK, D...  55.5 us
    pallas_call x1, Pallas kernels, qkv_back(): pl.pallas_call(kernel_qkv_back, out_shape=(jax.ShapeDtypeStruct((BLOCK, D...  31.5 us
    reduce_scatter x1, waiting for transfers between devices, body(): lax.psum_scatter(mm_tn(one_all, flat_grad).astype(bf), XZ, scatter_dimens...  31 us
    dot_general x4, matrix products, mm(): return jnp.dot(a, b, preferred_element_type=jnp.float32)  29.5 us
    ppermute x1, waiting for transfers between devices, body(): other_kv = lax.ppermute(own_kv, 'zh', swap)  26.2 us
    dot_general x5, matrix products, mm_tn(): lax.dot_general(a, b, (((0,), (0,)), ((), ())), preferred_element_type=jn...  26.2 us
  transfers between devices with their start and end apart: 9, of which 5 were waited for; matrix products, arithmetic and copies ran while one was open for 27% of the time, Pallas kernels for 26%

profile of v2, /device:TPU:1, one launch (start us, length us, event | category | flops | bytes accessed | tf_op | source)
XLA Modules:
  0.0 678.1 jit_solution(6367483947350316798)
XLA Ops:
  27.0 20.4 %spread.1 = (f32[16,8,1,128]{3,2,1,0:T(1,128)}, bf16[8,16,768]{2,1,0:T(8,128)(2,1)}, bf16[3,8,16,768]{3,2,1,0:T(8,128)(2,1)}, bf16[16,2048]{1,0:T(8,128)(2,1)}) custom-call(f32[1,128]{1,0:T(1,128)} %bitcast.334, bf16[8,16,768]{2,1,0:T(8,128)(2,1)} %reshape.464.qkv, bf16[8,3,16,768]{3,2,1,0:T(8,128)(2,1)} %pad_maximum_fusion.5.mlp, bf16[16,2048]{1,0:T(8,128)(2,1)} %reshape.469.out), custom_call_target="tpu_custom_call" | custom-call | tf_op jit(solution)/shard_map/spread/pallas_call | solution.py:556
  60.2 26.0 %norm_gather.1 = bf16[4,2,128,2048]{3,2,1,0:T(8,128)(2,1)} custom-call(bf16[128,2048]{1,0:T(8,128)(2,1)} %copy.149.hidden, f32[8,2048]{1,0:T(8,128)} %select_maximum_fusion.gains), custom_call_target="tpu_custom_call" | custom-call | tf_op jit(solution)/shard_map/norm_gather/pallas_call | solution.py:314
  86.2 12.2 %all-gather.4.cloned.1.call-done = bf16[2048,1024]{1,0:T(8,128)(2,1)} async-done(((bf16[128,1024]{1,0:T(8,128)(2,1)}), bf16[2048,1024]{1,0:T(8,128)(2,1)}) %all-gather.4.cloned.1.call-update) | async-done | bytes 4194320 | tf_op jit(solution)/shard_map/all_gather | solution.py:698
  98.4 8.2 %convolution_add_fusion = f32[1024,768]{1,0:T(8,128)} fusion(bf16[1024,2048]{1,0:T(8,128)(2,1)} %bitcast.278, f32[768]{0:T(1024)S(1)} %dynamic-slice_reduce_fusion, bf16[2048,1024]{1,0:T(8,128)(2,1)} %all-gather.4.cloned.1.call-done), kind=kOutput, calls=%fused_computation.31 | convolution fusion | flops 3222011904 | bytes 10488832 | tf_op jit(solution)/shard_map/dot_general | solution.py:92
  122.0 26.2 %collective-permute-done = bf16[2,2,512,4,64]{2,4,3,1,0:T(8,128)(2,1)S(1)} collective-permute-done((bf16[2,2,512,4,64]{2,4,3,1,0:T(8,128)(2,1)S(1)}, bf16[2,2,512,4,64]{2,4,3,1,0:T(8,128)(2,1)S(1)}, u32[]{:S(2)}, u32[]{:S(2)}) %collective-permute-start) | collective-permute-done | bytes 1048608 | tf_op jit(solution)/shard_map/ppermute | solution.py:753
  152.0 4.9 exponential_reduce_fusion
  158.3 5.6 fusion.10
  168.0 55.5 %out_proj.1 = (f32[128,2048]{1,0:T(8,128)}, bf16[4,2,128,2048]{3,2,1,0:T(8,128)(2,1)}) custom-call(bf16[4,2,128,256]{3,2,1,0:T(8,128)(2,1)} %bitcast.276, bf16[256,2048]{1,0:T(8,128)(2,1)} %bitcast.285, bf16[128,2048]{1,0:T(8,128)(2,1)} %copy.149.hidden, f32[8,2048]{1,0:T(8,128)} %select_maximum_fusion.gains), custom_call_target="tpu_custom_call" | custom-call | tf_op jit(solution)/shard_map/out_proj/pallas_call | solution.py:356
  223.6 6.3 fusion.29
  229.9 5.2 fusion.35
  235.1 5.1 fusion.34
  240.2 11.0 %multiply_convert_fusion.1 = (bf16[1024,768]{1,0:T(8,128)(2,1)}, bf16[1024,768]{1,0:T(8,128)(2,1)}, bf16[1024,768]{1,0:T(8,128)(2,1)S(1)}) fusion(f32[1024,768]{1,0:T(8,128)} %fusion.34, f32[1024,768]{1,0:T(8,128)} %fusion.35, bf16[1024,2048]{1,0:T(8,128)(2,1)} %all-gather.8.cloned.1.call-done, bf16[2048,768]{1,0:T(8,128)(2,1)} %bitcast.290), kind=kOutput, calls=%fused_computation.18 | convolution fusion | flops 3233021952 | bytes 18350080 | tf_op jit(solution)/shard_map/dot_general | solution.py:92
  252.4 5.1 convolution_convert_fusion
  257.6 64.7 %mlp_back.1 = (f32[128,2048]{1,0:T(8,128)}, f32[8,2048]{1,0:T(8,128)}, bf16[4,2,128,2048]{3,2,1,0:T(8,128)(2,1)}) custom-call(bf16[4,2,128,768]{3,2,1,0:T(8,128)(2,1)} %bitcast.309, bf16[4,2,128,768]{3,2,1,0:T(8,128)(2,1)} %bitcast.310, bf16[2048,768]{1,0:T(8,128)(2,1)} %bitcast.272, bf16[2048,768]{1,0:T(8,128)(2,1)} %bitcast.270, ...), custom_call_target="tpu_custom_call" | custom-call | tf_op jit(solution)/shard_map/mlp_back/pallas_call | solution.py:403
  322.3 4.3 convolution_convert_fusion.3
  330.7 13.1 %multiply_reduce_fusion = (f32[2,4,512]{2,1,0:T(4,128)S(1)}, f32[2,4,512,1024]{3,2,1,0:T(8,128)}) fusion(f32[2,4,512,1024]{3,2,1,0:T(8,128)} %copy-done, f32[2,4,512]{2,1,0:T(4,128)S(1)} %bitcast.325, pred[2,512,1024]{2,1,0:T(8,128)(4,1)S(1)} %and_and_fusion, bf16[2,512,4,64]{1,3,2,0:T(8,128)(2,1)} %reshape_reshape.18, ...), kind=kOutput, calls=%fused_computation.1 | convolution fusion | flops 557838336 | bytes 36208640 | tf_op jit(solution)/shard_map/gthd,gshd->ghts/dot_general | solution.py:802
  343.9 12.8 %multiply_convert_fusion = bf16[2,4,512,1024]{3,2,1,0:T(8,128)(2,1)S(1)} fusion(f32[2,4,512,1024]{3,2,1,0:T(8,128)} %get-tuple-element.129, f32[2,4,512,1024]{3,2,1,0:T(8,128)} %copy-done, f32[2,4,512]{2,1,0:T(4,128)S(1)} %get-tuple-element.128, f32[2,4,512]{2,1,0:T(4,128)S(1)} %bitcast.326, pred[2,512,1024]{2,1,0:T(8,128)(4,1)S(1)} %and_and_fusion), kind=kLoop, calls=%fused_computation | loop fusion | flops 25165824 | bytes 43024384 | tf_op jit(solution)/shard_map/convert_element_type | solution.py:805
  360.1 6.5 convolution_bitcast_fusion.1
  375.9 20.5 %collective-permute-done.1 = bf16[2,2,512,4,64]{2,4,3,1,0:T(8,128)(2,1)} collective-permute-done((bf16[2,2,512,4,64]{2,4,3,1,0:T(8,128)(2,1)}, bf16[2,2,512,4,64]{2,4,3,1,0:T(8,128)(2,1)}, u32[]{:S(2)}, u32[]{:S(2)}) %collective-permute-start.1) | collective-permute-done | bytes 1048608 | tf_op jit(solution)/shard_map/ppermute | solution.py:812
  401.2 8.0 %bitcast_convert_fusion = bf16[2048,768]{1,0:T(8,128)(2,1)} fusion(bf16[4,2,128,2048]{3,2,1,0:T(8,128)(2,1)} %norm_gather.1, bf16[2,4,128,768]{3,2,0,1:T(8,128)(2,1)S(1)} %copy.169), kind=kOutput, calls=%fused_computation.8 | convolution fusion | flops 3222798336 | bytes 8912896 | tf_op jit(solution)/shard_map/dot_general | solution.py:100
  409.3 6.9 %copy.174 = bf16[2048,1024]{1,0:T(8,128)(2,1)} copy(bf16[2048,1024]{0,1:T(8,128)(2,1)} %bitcast.279) | data formatting | bytes 8388608 | tf_op jit(solution)/shard_map/dot_general | solution.py:100
  416.2 6.3 convert_bitcast_fusion
  422.5 4.8 convert_bitcast_fusion.1
  427.3 4.9 convolution_convert_fusion.1
  432.1 6.9 %maximum_bitcast_fusion = bf16[16,3,128,768]{3,2,0,1:T(8,128)(2,1)} fusion(bf16[1,16,128,768]{3,2,1,0:T(8,128)(2,1)} %bitcast.292, bf16[1,16,128,768]{3,2,1,0:T(8,128)(2,1)S(1)} %convert_bitcast_fusion, bf16[1,16,128,768]{3,2,1,0:T(8,128)(2,1)} %convert_bitcast_fusion.1), kind=kLoop, calls=%fused_computation.6 | loop fusion | flops 9437184 | bytes 18874368 | tf_op jit(solution)/shard_map/transpose | solution.py:796
  439.0 8.4 %copy.175 = bf16[16,3,128,768]{3,2,1,0:T(8,128)(2,1)} copy(bf16[16,3,128,768]{3,2,0,1:T(8,128)(2,1)} %maximum_bitcast_fusion) | data formatting | bytes 18874368 | tf_op jit(solution)/shard_map/transpose | solution.py:796
  452.1 31.5 %qkv_back.1 = (f32[128,2048]{1,0:T(8,128)}, f32[8,2048]{1,0:T(8,128)}) custom-call(bf16[4,2,128,768]{3,2,1,0:T(8,128)(2,1)} %bitcast.268, bf16[2048,768]{1,0:T(8,128)(2,1)} %slice.235.weight, bf16[128,2048]{1,0:T(8,128)(2,1)} %copy.149.hidden, f32[128,2048]{1,0:T(8,128)} %get-tuple-element.34.middle_grad, f32[8,2048]{1,0:T(8,128)} %select_maximum_fusion.gains), custom_call_target="tpu_custom_call" | custom-call | tf_op jit(solution)/shard_map/qkv_back/pallas_call | solution.py:446
  494.0 31.0 %reduce-scatter.7.cloned.1.call-done = bf16[128,768]{1,0:T(8,128)(2,1)} async-done(((bf16[2048,768]{1,0:T(8,128)(2,1)}), bf16[128,768]{1,0:T(8,128)(2,1)}) %reduce-scatter.7.cloned.1.call-update) | async-done | bytes 196624 | tf_op jit(solution)/shard_map/reduce_scatter | solution.py:824
  525.0 91.4 %reduce-scatter.9.cloned.1.call-done = bf16[384,768]{1,0:T(8,128)(2,1)} async-done(((bf16[6144,768]{1,0:T(8,128)(2,1)}), bf16[384,768]{1,0:T(8,128)(2,1)}) %reduce-scatter.9.cloned.1.call-update) | async-done | bytes 589840 | tf_op jit(solution)/shard_map/reduce_scatter | solution.py:797
  616.4 18.1 %collect.1 = (f32[8,16,128]{2,1,0:T(8,128)}, bf16[8,16,768]{2,1,0:T(8,128)(2,1)}, bf16[8,3,16,768]{3,2,1,0:T(8,128)(2,1)}, bf16[16,2048]{1,0:T(8,128)(2,1)}) custom-call(f32[16,8,128]{2,1,0:T(8,128)} %pad.26.terms, f32[8,128]{1,0:T(8,128)} %pad.27.shift, bf16[8,16,768]{2,1,0:T(8,128)(2,1)} %bitcast.322, bf16[3,8,16,768]{3,2,1,0:T(8,128)(2,1)} %bitcast.317, ...), custom_call_target="tpu_custom_call" | custom-call | tf_op jit(solution)/shard_map/collect/pallas_call | solution.py:623
  636.4 5.4 reshape.509
  664.3 5.5 reshape.500
  (258 shorter events, 119.2 us)
Async XLA Ops:
  7.2 8.8 %copy-start.27 = (bf16[16,6144]{1,0:T(8,128)(2,1)S(1)}, bf16[16,6144]{1,0:T(8,128)(2,1)}, u32[]{:S(2)}) copy-start(bf16[16,6144]{1,0:T(8,128)(2,1)} %param.20) | copy-start | bytes 589828
  7.2 91.2 %all-gather.4.cloned.1.call-start = ((), (), s32[]{:S(2)}) async-start(), calls=%async_computation.4 | async-start | bytes 4456448 | tf_op jit(solution)/shard_map/all_gather | solution.py:698
  18.1 8.2 %copy-start.32 = (bf16[16]{0:T(256)(128)(2,1)S(1)}, bf16[16]{0:T(256)(128)(2,1)}, u32[]{:S(2)}) copy-start(bf16[16]{0:T(256)(128)(2,1)} %param.18) | copy-start | bytes 100
  18.1 8.2 %copy-start.33 = (bf16[16]{0:T(256)(128)(2,1)S(1)}, bf16[16]{0:T(256)(128)(2,1)}, u32[]{:S(2)}) copy-start(bf16[16]{0:T(256)(128)(2,1)} %param.19) | copy-start | bytes 100
  18.1 8.2 %copy-start.34 = (bf16[16]{0:T(256)(128)(2,1)S(1)}, bf16[16]{0:T(256)(128)(2,1)}, u32[]{:S(2)}) copy-start(bf16[16]{0:T(256)(128)(2,1)} %param.23) | copy-start | bytes 100
  18.1 8.2 %copy-start.35 = (bf16[16]{0:T(256)(128)(2,1)S(1)}, bf16[16]{0:T(256)(128)(2,1)}, u32[]{:S(2)}) copy-start(bf16[16]{0:T(256)(128)(2,1)} %param.24) | copy-start | bytes 100
  22.3 28.5 %copy-start.31 = (s32[1,2]{1,0:T(1,128)S(1)}, s32[1,2]{1,0:T(1,128)}, u32[]{:S(2)}) copy-start(s32[1,2]{1,0:T(1,128)} %param.16) | copy-start | bytes 28
  22.3 29.8 %copy-start.24 = (bf16[1,128,2048]{2,1,0:T(8,128)(2,1)S(1)}, bf16[1,128,2048]{2,1,0:T(8,128)(2,1)}, u32[]{:S(2)}) copy-start(bf16[1,128,2048]{2,1,0:T(8,128)(2,1)} %param.15) | copy-start | bytes 1572868
  25.4 27.2 %copy-start.39 = (s32[8]{0:T(128)S(1)}, s32[8]{0:T(128)}, u32[]{:S(2)}) copy-start(s32[8]{0:T(128)} %get-tuple-element.122) | copy-start | bytes 100
  48.3 7.1 %copy-start.19 = (f32[16,8,1,128]{3,2,1,0:T(1,128)S(1)}, f32[16,8,1,128]{3,2,1,0:T(1,128)}, u32[]{:S(2)}) copy-start(f32[16,8,1,128]{3,2,1,0:T(1,128)} %get-tuple-element.27) | copy-start | bytes 196612
  50.0 173.6 %all-gather.6.cloned.1.call-start = ((), (), s32[]{:S(2)}) async-start(), calls=%async_computation.5 | async-start | bytes 10027008 | tf_op jit(solution)/shard_map/all_gather | solution.py:701
  50.7 189.5 %all-gather.8.cloned.1.call-start = ((), (), s32[]{:S(2)}) async-start(), calls=%async_computation.7 | async-start | bytes 4718592 | tf_op jit(solution)/shard_map/all_gather | solution.py:744
  55.0 436.4 %reduce-scatter.5.cloned.1.call-start = ((), (), s32[]{:S(2)}) async-start(), calls=%async_computation.6 | async-start | bytes 4718592 | tf_op jit(solution)/shard_map/reduce_scatter | solution.py:772
  116.0 32.5 %copy-start.26 = (bf16[2,512,4,8]{1,3,2,0:T(8,128)(2,1)}, bf16[2,512,4,8]{1,3,2,0:T(8,128)(2,1)S(1)}, u32[]{:S(2)}) copy-start(bf16[2,512,4,8]{1,3,2,0:T(8,128)(2,1)S(1)} %get-tuple-element.97) | copy-start | bytes 196612
  116.2 32.1 %collective-permute-start = (bf16[2,2,512,4,64]{2,4,3,1,0:T(8,128)(2,1)S(1)}, bf16[2,2,512,4,64]{2,4,3,1,0:T(8,128)(2,1)S(1)}, u32[]{:S(2)}, u32[]{:S(2)}) collective-permute-start(bf16[2,2,512,4,64]{2,4,3,1,0:T(8,128)(2,1)S(1)} %pad_maximum_fusion.4), channel_id=1, source_target_pairs={{0,64},{64,0},{1,65},{65,1},{2,66},{66,2},{3,67},{67,3},{4,68},{68... | collective-permute-start | bytes 3145736 | tf_op jit(solution)/shard_map/ppermute | solution.py:753
  120.2 223.7 %copy-start.1 = (pred[2,512,1024]{2,1,0:T(8,128)(4,1)}, pred[2,512,1024]{2,1,0:T(8,128)(4,1)S(1)}, u32[]{:S(2)}) copy-start(pred[2,512,1024]{2,1,0:T(8,128)(4,1)S(1)} %and_and_fusion) | copy-start | bytes 3145732
  120.3 28.2 %copy-start.22 = (bf16[2,512,4,48]{1,3,2,0:T(8,128)(2,1)}, bf16[2,512,4,48]{1,3,2,0:T(8,128)(2,1)S(1)}, u32[]{:S(2)}) copy-start(bf16[2,512,4,48]{1,3,2,0:T(8,128)(2,1)S(1)} %slice.324) | copy-start | bytes 1179652
  148.5 182.2 %copy-start.7 = (bf16[2,2,1024,4,64]{2,4,3,1,0:T(8,128)(2,1)}, bf16[2,2,1024,4,64]{2,4,3,1,0:T(8,128)(2,1)S(1)}, u32[]{:S(2)}) copy-start(bf16[2,2,1024,4,64]{2,4,3,1,0:T(8,128)(2,1)S(1)} %pad_maximum_fusion.2) | copy-start | bytes 6291460
  156.8 187.0 %copy-start.28 = (f32[1,8,512]{2,1,0:T(8,128)}, f32[1,8,512]{2,1,0:T(8,128)S(1)}, u32[]{:S(2)}) copy-start(f32[1,8,512]{2,1,0:T(8,128)S(1)} %log_add_fusion) | copy-start | bytes 49156
  240.2 12.2 %copy-start.17 = (bf16[16,1,128,768]{3,2,0,1:T(8,128)(2,1)S(1)}, bf16[16,1,128,768]{3,2,0,1:T(8,128)(2,1)}, u32[]{:S(2)}) copy-start(bf16[16,1,128,768]{3,2,0,1:T(8,128)(2,1)} %get-tuple-element.84) | copy-start | bytes 9437188
  257.5 236.5 %reduce-scatter.11.cloned.1.call-start = ((), (), s32[]{:S(2)}) async-start(), calls=%async_computation.10 | async-start | bytes 1114112 | tf_op jit(solution)/shard_map/reduce_scatter | solution.py:799
  257.6 64.7 %copy-start.14 = (bf16[32,8,8,256]{3,1,2,0:T(8,128)(2,1)S(1)}, bf16[32,8,8,256]{3,1,2,0:T(8,128)(2,1)}, u32[]{:S(2)}) copy-start(bf16[32,8,8,256]{3,1,2,0:T(8,128)(2,1)} %copy.200) | copy-start | bytes 3145732
  343.9 15.9 %slice-start = ((s8[16777216]{0:T(1024)(128)(4,1)}), s8[4194304]{0:T(1024)(128)(4,1)S(1)}, s32[]{:S(2)}) async-start(s8[16777216]{0:T(1024)(128)(4,1)} %bitcast.265), calls=%async_computation.11 | async-start | bytes 8388608
  343.9 15.9 %slice-start.1 = ((s8[16777216]{0:T(1024)(128)(4,1)}), s8[4194304]{0:T(1024)(128)(4,1)S(1)}, s32[]{:S(2)}) async-start(s8[16777216]{0:T(1024)(128)(4,1)} %bitcast.265), calls=%async_computation.12 | async-start | bytes 8388608
  343.9 15.9 %slice-start.2 = ((s8[16777216]{0:T(1024)(128)(4,1)}), s8[4194304]{0:T(1024)(128)(4,1)S(1)}, s32[]{:S(2)}) async-start(s8[16777216]{0:T(1024)(128)(4,1)} %bitcast.265), calls=%async_computation.13 | async-start | bytes 8388608
  369.0 27.4 %collective-permute-start.1 = (bf16[2,2,512,4,64]{2,4,3,1,0:T(8,128)(2,1)}, bf16[2,2,512,4,64]{2,4,3,1,0:T(8,128)(2,1)}, u32[]{:S(2)}, u32[]{:S(2)}) collective-permute-start(bf16[2,2,512,4,64]{2,4,3,1,0:T(8,128)(2,1)} %fusion.6), channel_id=1, source_target_pairs={{0,64},{64,0},{1,65},{65,1},{2,66},{66,2},{3,67},{67,3},{4,68},{68... | collective-permute-start | bytes 3145736 | tf_op jit(solution)/shard_map/ppermute | solution.py:812
  375.8 22.6 %copy-start.29 = (f32[2,512,8]{1,2,0:T(8,128)S(1)}, f32[2,512,8]{1,2,0:T(8,128)}, u32[]{:S(2)}) copy-start(f32[2,512,8]{1,2,0:T(8,128)} %get-tuple-element.113) | copy-start | bytes 98308
  375.8 149.2 %reduce-scatter.7.cloned.1.call-start = ((), (), s32[]{:S(2)}) async-start(), calls=%async_computation.8 | async-start | bytes 3342336 | tf_op jit(solution)/shard_map/reduce_scatter | solution.py:824
  401.2 8.0 %copy-start.3 = (bf16[2,4,128,768]{3,2,0,1:T(8,128)(2,1)}, bf16[2,4,128,768]{3,2,0,1:T(8,128)(2,1)S(1)}, u32[]{:S(2)}) copy-start(bf16[2,4,128,768]{3,2,0,1:T(8,128)(2,1)S(1)} %copy.169) | copy-start | bytes 4718596
  409.3 207.2 %reduce-scatter.9.cloned.1.call-start = ((), (), s32[]{:S(2)}) async-start(), calls=%async_computation.9 | async-start | bytes 10027008 | tf_op jit(solution)/shard_map/reduce_scatter | solution.py:797
  649.4 10.6 %copy-start.15 = (f32[16,1,2,4,4,2,2,16]{7,5,6,4,1,0,2,3:T(2,128)S(1)}, f32[16,1,2,4,4,2,2,16]{7,5,6,4,1,0,2,3:T(2,128)}, u32[]{:S(2)}) copy-start(f32[16,1,2,4,4,2,2,16]{7,5,6,4,1,0,2,3:T(2,128)} %slice_bitcast_fusion) | copy-start | bytes 393220
  651.3 9.3 %copy-start.9 = (f32[16,2,2,4,4,2,2,16]{7,6,5,4,1,0,2,3:T(2,128)S(1)}, f32[16,2,2,4,4,2,2,16]{7,6,5,4,1,0,2,3:T(2,128)}, u32[]{:S(2)}) copy-start(f32[16,2,2,4,4,2,2,16]{7,6,5,4,1,0,2,3:T(2,128)} %slice.262) | copy-start | bytes 786436
  (25 other events, 108.5 us)
Sparse Core Ops, SparseCore 0:
  50.1 48.2 all-gather.3
  100.5 96.7 all-gather.5
  199.1 35.7 all-gather.7
  257.7 43.7 reduce-scatter.4
  376.0 70.4 reduce-scatter.10
  450.0 74.9 reduce-scatter.6
  528.9 87.4 reduce-scatter.8
